TPU v7x, 128 devices: a whole 4x4x4 slice. The times are simulated.
128 devices in a mesh: ctx: 32 (over x, y, core), kvh: 4 (over z).
Axes of the slice: x: 4, y: 4, z: 4, core: 2. Of those that a mesh axis runs over, the one named last changes fastest.
Arguments:
- queries: bfloat16 [49152, 2048], P('ctx', 'kvh'), may hold values from -44 to 44
- key_rows: bfloat16 [49152, 512], P('ctx', 'kvh'), may hold values from -10 to 10
- value_rows: bfloat16 [49152, 512], P('ctx', 'kvh'), may hold values from -6 to 6
- out_grad: bfloat16 [49152, 2048], P('ctx', 'kvh'), may hold values from -6 to 6
- picked: int32 [96, 2], replicated, may hold values from 0 to 95, as said below
Outputs:
- query_grad: bfloat16 [49152, 2048], P(('ctx', 'kvh'))
- key_grad: bfloat16 [49152, 512], P(('ctx', 'kvh'))
- value_grad: bfloat16 [49152, 512], P(('ctx', 'kvh'))
Inputs may be any that keep to these rules, and one draw needn't show every extreme that they name: `picked`: row q names key blocks before q, or q itself for no pick; the two differ unless both are q. All picks of the 3 query blocks of one index of ctx that lie in blocks of another index name one and the same block of that index. The last block's second pick is dead.
All inputs are finite; a program needn't handle non-finite values.
Results may differ from a plain program's by a relative error of at most 0.0096.
Values may be sent and summed in bfloat16 or wider, within the bound.
A program may use at most 192 MiB of HBM per device.

v0:
```python
import jax
import jax.numpy as jnp
from jax import lax
from jax.sharding import PartitionSpec as P

HEAD = 128
BLK = 512


def tile_grads(query_tile, grad_tile, key_tiles, value_tiles, alive_mask):
    block_len = query_tile.shape[0]
    scaling = 1.0 / HEAD**0.5
    scores = (
        jnp.einsum("acgd,jbcd->acgjb", query_tile, key_tiles, preferred_element_type=jnp.float32)
        * scaling
    )
    row_ids = jnp.arange(block_len)
    causal = row_ids[None, :] <= row_ids[:, None]
    first_pick = jnp.arange(key_tiles.shape[0]) == 0
    allowed = jnp.where(first_pick[None, :, None], causal[:, None, :], alive_mask[None, :, None])
    scores = jnp.where(allowed[:, None, None, :, :], scores, -jnp.inf)
    row_top = jnp.max(scores, axis=(3, 4), keepdims=True)
    log_total = row_top + jnp.log(jnp.sum(jnp.exp(scores - row_top), axis=(3, 4), keepdims=True))
    weights = jnp.exp(scores - log_total)
    weights_low = weights.astype(jnp.bfloat16)
    attn_out = jnp.einsum(
        "acgjb,jbcd->acgd", weights_low, value_tiles, preferred_element_type=jnp.float32
    )
    row_delta = jnp.sum(grad_tile.astype(jnp.float32) * attn_out, axis=-1)
    weight_grad = jnp.einsum(
        "acgd,jbcd->acgjb", grad_tile, value_tiles, preferred_element_type=jnp.float32
    )
    score_grad = (weights * (weight_grad - row_delta[..., None, None]) * scaling).astype(
        jnp.bfloat16
    )
    query_part = jnp.einsum(
        "acgjb,jbcd->acgd", score_grad, key_tiles, preferred_element_type=jnp.float32
    ).astype(jnp.bfloat16)
    key_part = jnp.einsum(
        "acgjb,acgd->jbcd", score_grad, query_tile, preferred_element_type=jnp.float32
    )
    value_part = jnp.einsum(
        "acgjb,acgd->jbcd", weights_low, grad_tile, preferred_element_type=jnp.float32
    )
    return (query_part, key_part, value_part)


def per_block(members):
    return tile_grads(members[0], members[1], members[2], members[3], members[4])


def per_device(queries, key_rows, value_rows, out_grad, picked):
    cycle_size = lax.axis_size("ctx")
    my_index = lax.axis_index("ctx")
    block_count = key_rows.shape[0] // BLK
    row_width = key_rows.shape[1]
    kv_local = row_width // HEAD
    group_size = queries.shape[1] // row_width
    key_blocks = key_rows.reshape(block_count, BLK, row_width)
    value_blocks = value_rows.reshape(block_count, BLK, row_width)
    total_blocks = picked.shape[0]
    block_ids = jnp.arange(total_blocks)
    owners = picked // block_count
    askers = jnp.broadcast_to((block_ids // block_count)[:, None], picked.shape)
    remote = (picked != block_ids[:, None]) & (owners != askers)
    devices = jnp.arange(cycle_size)
    flat_pick = picked.reshape(-1)
    matches = (
        (askers.reshape(-1)[:, None, None] == devices[None, :, None])
        & (owners.reshape(-1)[:, None, None] == devices[None, None, :])
        & remote.reshape(-1)[:, None, None]
    )
    needed = jnp.max(jnp.where(matches, flat_pick[:, None, None] + 1, 0), axis=0)
    wanted = needed[:, my_index] - 1 - my_index * block_count
    chooser = wanted[:, None] == jnp.arange(block_count)[None, :]
    chooser_low = chooser.astype(jnp.bfloat16)
    key_send = (
        jnp.dot(
            chooser_low, key_blocks.reshape(block_count, -1), preferred_element_type=jnp.float32
        )
        .astype(jnp.bfloat16)
        .reshape(cycle_size, BLK, row_width)
    )
    value_send = (
        jnp.dot(
            chooser_low, value_blocks.reshape(block_count, -1), preferred_element_type=jnp.float32
        )
        .astype(jnp.bfloat16)
        .reshape(cycle_size, BLK, row_width)
    )
    got_keys, got_values = (
        lax.all_to_all(key_send, "ctx", split_axis=0, concat_axis=0, tiled=True),
        lax.all_to_all(value_send, "ctx", split_axis=0, concat_axis=0, tiled=True),
    )
    own_picks = lax.dynamic_slice_in_dim(picked, my_index * block_count, block_count, 0)
    own_ids = my_index * block_count + jnp.arange(block_count)
    all_ids = jnp.concatenate([own_ids[:, None], own_picks], axis=1)
    alive_mask = jnp.concatenate(
        [jnp.ones((block_count, 1), bool), own_picks != own_ids[:, None]], axis=1
    )
    holder = all_ids // block_count
    source = jnp.where(holder == my_index, all_ids - my_index * block_count, block_count + holder)
    flat_source = source.reshape(-1)
    slot_count = block_count + cycle_size
    key_table = jnp.concatenate([key_blocks, got_keys], axis=0)
    value_table = jnp.concatenate([value_blocks, got_values], axis=0)
    key_tiles = jnp.take(key_table, flat_source, axis=0)
    value_tiles = jnp.take(value_table, flat_source, axis=0)
    picks_per = all_ids.shape[1]
    key_tiles = key_tiles.reshape(block_count, picks_per, BLK, kv_local, HEAD)
    value_tiles = value_tiles.reshape(block_count, picks_per, BLK, kv_local, HEAD)
    query_blocks = queries.reshape(block_count, BLK, kv_local, group_size, HEAD)
    grad_blocks = out_grad.reshape(block_count, BLK, kv_local, group_size, HEAD)
    query_parts, key_parts, value_parts = lax.map(
        per_block, (query_blocks, grad_blocks, key_tiles, value_tiles, alive_mask)
    )
    spread = (flat_source[:, None] == jnp.arange(slot_count)[None, :]).astype(jnp.float32)
    key_sums = jnp.dot(
        spread.T,
        key_parts.reshape(block_count * picks_per, -1),
        precision=lax.Precision.HIGHEST,
        preferred_element_type=jnp.float32,
    )
    value_sums = jnp.dot(
        spread.T,
        value_parts.reshape(block_count * picks_per, -1),
        precision=lax.Precision.HIGHEST,
        preferred_element_type=jnp.float32,
    )
    back_keys = key_sums[block_count:].reshape(cycle_size, BLK, row_width)
    back_values = value_sums[block_count:].reshape(cycle_size, BLK, row_width)
    came_keys, came_values = (
        lax.all_to_all(back_keys, "ctx", split_axis=0, concat_axis=0, tiled=True),
        lax.all_to_all(back_values, "ctx", split_axis=0, concat_axis=0, tiled=True),
    )
    gather_in = chooser.astype(jnp.float32)
    key_total = key_sums[:block_count] + jnp.dot(
        gather_in.T,
        came_keys.reshape(cycle_size, -1),
        precision=lax.Precision.HIGHEST,
        preferred_element_type=jnp.float32,
    )
    value_total = value_sums[:block_count] + jnp.dot(
        gather_in.T,
        came_values.reshape(cycle_size, -1),
        precision=lax.Precision.HIGHEST,
        preferred_element_type=jnp.float32,
    )
    query_local = query_parts.reshape(block_count * BLK, queries.shape[1])
    key_local = key_total.reshape(block_count * BLK, row_width).astype(jnp.bfloat16)
    value_local = value_total.reshape(block_count * BLK, row_width).astype(jnp.bfloat16)
    query_out, key_out, value_out = (
        lax.all_to_all(query_local, "kvh", split_axis=0, concat_axis=1, tiled=True),
        lax.all_to_all(key_local, "kvh", split_axis=0, concat_axis=1, tiled=True),
        lax.all_to_all(value_local, "kvh", split_axis=0, concat_axis=1, tiled=True),
    )
    return (query_out, key_out, value_out)


def solution(mesh):
    return jax.shard_map(
        per_device,
        mesh=mesh,
        in_specs=(P("ctx", "kvh"), P("ctx", "kvh"), P("ctx", "kvh"), P("ctx", "kvh"), P()),
        out_specs=(P(("ctx", "kvh"), None), P(("ctx", "kvh"), None), P(("ctx", "kvh"), None)),
        check_vma=False,
    )
```

profile of v0, /device:TPU:8, one launch (start us, length us, event | category | flops | bytes accessed | tf_op | source)
XLA Modules:
  0.0 580.5 jit_solution(9837209749592798600)
XLA Ops:
  9.2 7.7 %all-to-all-start = ((bf16[32,512,128]{2,1,0:T(8,128)(2,1)}), bf16[32,512,128]{2,1,0:T(8,128)(2,1)}, u32[]{:S(2)}, u32[]{:S(2)}) async-start(bf16[32,512,128]{2,1,0:T(8,128)(2,1)} %bitcast.248), calls=%async_computation | async-start | bytes 8388608 | tf_op jit(solution)/shard_map/all_to_all | solution.py:92
  21.4 50.1 %all-to-all-done = bf16[32,512,128]{2,1,0:T(8,128)(2,1)} async-done(((bf16[32,512,128]{2,1,0:T(8,128)(2,1)}), bf16[32,512,128]{2,1,0:T(8,128)(2,1)}, u32[]{:S(2)}, u32[]{:S(2)}) %all-to-all-start) | async-done | bytes 4194336 | tf_op jit(solution)/shard_map/all_to_all | solution.py:92
  71.5 4.9 all-to-all-start.1
  83.1 4.7 pad_maximum_fusion
  90.8 40.0 %all-to-all-done.1 = bf16[32,512,128]{2,1,0:T(8,128)(2,1)} async-done(((bf16[32,512,128]{2,1,0:T(8,128)(2,1)}), bf16[32,512,128]{2,1,0:T(8,128)(2,1)}, u32[]{:S(2)}, u32[]{:S(2)}) %all-to-all-start.1) | async-done | bytes 4194336 | tf_op jit(solution)/shard_map/all_to_all | solution.py:93
  142.2 115.6 %while.14 = (s32[]{:T(128)}, bf16[3,512,1,4,128]{4,3,1,0,2:T(4,128)(2,1)}, f32[3,3,512,1,128]{4,2,1,0,3:T(8,128)}, f32[3,3,512,1,128]{4,2,1,0,3:T(8,128)}, bf16[...) while((s32[]{:T(128)}, ...), condition=%wide.region_5.7_spmd, body=%wide.region_1.6_spmd.sunk | while | flops 4903137280 | bytes 240216864 | solution.py:114
  155.1 8.4 %fusion.76 = f32[512,4]{0,1:T(4,128)S(1)} fusion(bf16[1,512,1,4,128]{1,4,3,2,0:T(8,128)(2,1)S(1)} %copy.184, bf16[3,3,512,1,128]{4,2,1,3,0:T(8,128)(2,1)} %get-tuple-element.223, s32[]{:T(128)} %get-tuple-element.206, f32[3,512,512,4]{2,1,3,0:T(8,128)} %copy-done, f32[512,4]{0,1:T(4,128)S(1)} %log_add_fusion.2, ...), kind=kOutput, calls=%fused_computation.20.clone.1 | convolution fusion | flops 818673664 | bytes 14303744 | tf_op jit(solution)/shard_map/while/body/eval_jaxpr/acgjb,jbcd->acgd/dot_general | solution.py:26
  163.5 5.6 fusion.77
  193.5 8.4 %fusion.76 = f32[512,4]{0,1:T(4,128)S(1)} fusion(bf16[1,512,1,4,128]{1,4,3,2,0:T(8,128)(2,1)S(1)} %copy.184, bf16[3,3,512,1,128]{4,2,1,3,0:T(8,128)(2,1)} %get-tuple-element.223, s32[]{:T(128)} %get-tuple-element.206, f32[3,512,512,4]{2,1,3,0:T(8,128)} %copy-done, f32[512,4]{0,1:T(4,128)S(1)} %log_add_fusion.2, ...), kind=kOutput, calls=%fused_computation.20.clone.1 | convolution fusion | flops 818673664 | bytes 14303744 | tf_op jit(solution)/shard_map/while/body/eval_jaxpr/acgjb,jbcd->acgd/dot_general | solution.py:26
  201.9 5.6 fusion.77
  231.9 8.4 %fusion.76 = f32[512,4]{0,1:T(4,128)S(1)} fusion(bf16[1,512,1,4,128]{1,4,3,2,0:T(8,128)(2,1)S(1)} %copy.184, bf16[3,3,512,1,128]{4,2,1,3,0:T(8,128)(2,1)} %get-tuple-element.223, s32[]{:T(128)} %get-tuple-element.206, f32[3,512,512,4]{2,1,3,0:T(8,128)} %copy-done, f32[512,4]{0,1:T(4,128)S(1)} %log_add_fusion.2, ...), kind=kOutput, calls=%fused_computation.20.clone.1 | convolution fusion | flops 818673664 | bytes 14303744 | tf_op jit(solution)/shard_map/while/body/eval_jaxpr/acgjb,jbcd->acgd/dot_general | solution.py:26
  240.3 5.6 fusion.77
  266.2 5.3 all-to-all-start.2
  271.5 6.4 %fusion.36 = f32[35,65536]{1,0:T(8,128)S(1)} fusion(f32[9,65536]{1,0:T(8,128)} %bitcast.245, s32[9]{0:T(128)S(1)} %copy-done.16), kind=kOutput, calls=%fused_computation.75 | convolution fusion | flops 247726400 | bytes 11534372 | tf_op jit(solution)/shard_map/dot_general | solution.py:124
  281.9 4.8 copy.149
  286.7 5.5 all-to-all-done.2
  292.2 5.6 all-to-all-start.5
  308.9 4.7 copy.146
  313.6 108.1 %all-to-all-done.5 = f32[32,512,128]{2,1,0:T(8,128)} async-done(((f32[32,512,128]{2,1,0:T(8,128)}), f32[32,512,128]{2,1,0:T(8,128)}, u32[]{:S(2)}, u32[]{:S(2)}) %all-to-all-start.5) | async-done | bytes 8388640 | tf_op jit(solution)/shard_map/all_to_all | solution.py:134
  421.7 5.8 all-to-all-start.3
  427.5 11.0 %fusion.29 = bf16[3,65536]{1,0:T(4,128)(2,1)S(1)} fusion(f32[4,8,512,128]{3,2,1,0:T(8,128)} %bitcast.100, f32[35,65536]{1,0:T(8,128)} %copy-done.3, s32[32]{0:T(128)S(1)} %copy-done.13), kind=kOutput, calls=%fused_computation.54 | convolution fusion | flops 75890784 | bytes 9568384 | tf_op jit(solution)/shard_map/dot_general | solution.py:143
  439.8 111.6 %all-to-all-done.3 = f32[32,512,128]{2,1,0:T(8,128)} async-done(((f32[32,512,128]{2,1,0:T(8,128)}), f32[32,512,128]{2,1,0:T(8,128)}, u32[]{:S(2)}, u32[]{:S(2)}) %all-to-all-start.3) | async-done | bytes 8388640 | tf_op jit(solution)/shard_map/all_to_all | solution.py:133
  554.9 11.0 %fusion.28 = bf16[3,65536]{1,0:T(4,128)(2,1)S(1)} fusion(f32[4,8,512,128]{3,2,1,0:T(8,128)} %bitcast.91, f32[35,65536]{1,0:T(8,128)} %copy-done.4, s32[32]{0:T(128)S(1)} %copy-done.13), kind=kOutput, calls=%fused_computation.53 | convolution fusion | flops 75890784 | bytes 9568384 | tf_op jit(solution)/shard_map/dot_general | solution.py:137
  567.2 4.7 all-to-all-start.4
  (168 shorter events, 144.7 us)
Async XLA Ops:
  5.0 12.1 %copy-start.12 = (s32[32]{0:T(128)}, s32[32]{0:T(128)S(1)}, u32[]{:S(2)}) copy-start(s32[32]{0:T(128)S(1)} %subtract_reduce_fusion) | copy-start | bytes 388
  9.2 7.7 %copy-start.9 = (bf16[1536,128]{1,0:T(8,128)(2,1)S(1)}, bf16[1536,128]{1,0:T(8,128)(2,1)}, u32[]{:S(2)}) copy-start(bf16[1536,128]{1,0:T(8,128)(2,1)} %param.11) | copy-start | bytes 1179652
  9.2 62.3 %all-to-all-start = ((bf16[32,512,128]{2,1,0:T(8,128)(2,1)}), bf16[32,512,128]{2,1,0:T(8,128)(2,1)}, u32[]{:S(2)}, u32[]{:S(2)}) async-start(bf16[32,512,128]{2,1,0:T(8,128)(2,1)} %bitcast.248), calls=%async_computation | async-start | bytes 8388608 | tf_op jit(solution)/shard_map/all_to_all | solution.py:92
  21.4 55.0 %copy-start.14 = (s32[96,2]{0,1:T(2,128)S(1)}, s32[96,2]{0,1:T(2,128)}, u32[]{:S(2)}) copy-start(s32[96,2]{0,1:T(2,128)} %param.13) | copy-start | bytes 2308
  21.4 55.6 %copy-start.10 = (bf16[1536,512]{1,0:T(8,128)(2,1)S(1)}, bf16[1536,512]{1,0:T(8,128)(2,1)}, u32[]{:S(2)}) copy-start(bf16[1536,512]{1,0:T(8,128)(2,1)} %param.9) | copy-start | bytes 4718596
  71.5 59.4 %all-to-all-start.1 = ((bf16[32,512,128]{2,1,0:T(8,128)(2,1)}), bf16[32,512,128]{2,1,0:T(8,128)(2,1)}, u32[]{:S(2)}, u32[]{:S(2)}) async-start(bf16[32,512,128]{2,1,0:T(8,128)(2,1)} %bitcast.247), calls=%async_computation.1 | async-start | bytes 8388608 | tf_op jit(solution)/shard_map/all_to_all | solution.py:93
  76.3 6.8 %copy-start.8 = (bf16[1536,128]{1,0:T(8,128)(2,1)S(1)}, bf16[1536,128]{1,0:T(8,128)(2,1)}, u32[]{:S(2)}) copy-start(bf16[1536,128]{1,0:T(8,128)(2,1)} %param.10) | copy-start | bytes 1179652
  146.4 4.5 copy-start
  155.1 8.4 %copy-start.1 = (f32[3,512,512,4]{2,1,3,0:T(8,128)S(1)}, f32[3,512,512,4]{2,1,3,0:T(8,128)}, u32[]{:S(2)}) copy-start(f32[3,512,512,4]{2,1,3,0:T(8,128)} %copy-done) | copy-start | bytes 37748740 | tf_op jit(solution)/shard_map/while
  175.5 5.3 copy-start.6
  184.8 4.5 copy-start
  193.5 8.4 %copy-start.1 = (f32[3,512,512,4]{2,1,3,0:T(8,128)S(1)}, f32[3,512,512,4]{2,1,3,0:T(8,128)}, u32[]{:S(2)}) copy-start(f32[3,512,512,4]{2,1,3,0:T(8,128)} %copy-done) | copy-start | bytes 37748740 | tf_op jit(solution)/shard_map/while
  213.9 5.3 copy-start.6
  223.2 4.5 copy-start
  231.9 8.4 %copy-start.1 = (f32[3,512,512,4]{2,1,3,0:T(8,128)S(1)}, f32[3,512,512,4]{2,1,3,0:T(8,128)}, u32[]{:S(2)}) copy-start(f32[3,512,512,4]{2,1,3,0:T(8,128)} %copy-done) | copy-start | bytes 37748740 | tf_op jit(solution)/shard_map/while
  252.3 5.3 copy-start.6
  264.2 7.3 %copy-start.16 = (s32[9]{0:T(128)S(1)}, s32[9]{0:T(128)}, u32[]{:S(2)}) copy-start(s32[9]{0:T(128)} %copy-done.15) | copy-start | bytes 112
  266.2 26.0 %all-to-all-start.2 = ((bf16[4,384,512]{2,1,0:T(8,128)(2,1)}), bf16[4,384,512]{2,1,0:T(8,128)(2,1)}, u32[]{:S(2)}, u32[]{:S(2)}) async-start(bf16[4,384,512]{2,1,0:T(8,128)(2,1)} %all_to_all.52), calls=%async_computation.2 | async-start | bytes 3145728 | tf_op jit(solution)/shard_map/all_to_all | solution.py:153
  292.2 5.6 copy-start.7
  292.2 129.5 %all-to-all-start.5 = ((f32[32,512,128]{2,1,0:T(8,128)}), f32[32,512,128]{2,1,0:T(8,128)}, u32[]{:S(2)}, u32[]{:S(2)}) async-start(f32[32,512,128]{2,1,0:T(8,128)} %bitcast.242), calls=%async_computation.5 | async-start | bytes 16777216 | tf_op jit(solution)/shard_map/all_to_all | solution.py:134
  421.7 5.8 copy-start.13
  421.7 129.7 %all-to-all-start.3 = ((f32[32,512,128]{2,1,0:T(8,128)}), f32[32,512,128]{2,1,0:T(8,128)}, u32[]{:S(2)}, u32[]{:S(2)}) async-start(f32[32,512,128]{2,1,0:T(8,128)} %bitcast.243), calls=%async_computation.3 | async-start | bytes 16777216 | tf_op jit(solution)/shard_map/all_to_all | solution.py:133
  551.4 15.8 %all-to-all-start.6 = ((bf16[4,384,128]{2,1,0:T(8,128)(2,1)}), bf16[4,384,128]{2,1,0:T(8,128)(2,1)S(1)}, u32[]{:S(2)}, u32[]{:S(2)}) async-start(bf16[4,384,128]{2,1,0:T(8,128)(2,1)} %convert_element_type.57), calls=%async_computation.6 | async-start | bytes 786432 | tf_op jit(solution)/shard_map/all_to_all | solution.py:155
  567.2 12.3 %all-to-all-start.4 = ((bf16[4,384,128]{2,1,0:T(8,128)(2,1)}), bf16[4,384,128]{2,1,0:T(8,128)(2,1)S(1)}, u32[]{:S(2)}, u32[]{:S(2)}) async-start(bf16[4,384,128]{2,1,0:T(8,128)(2,1)} %convert_element_type.55), calls=%async_computation.4 | async-start | bytes 786432 | tf_op jit(solution)/shard_map/all_to_all | solution.py:154
  (10 other events, 32.7 us)
where the time goes:
time: 588 us; the launch traced here: 581 us
  waiting for transfers between devices  319 us (54%)
  matrix products  113 us (19%)
  local copies, waits for them, and re-layouts  85 us (14%)
  starting transfers between devices  37.4 us (6%)
  other arithmetic  24.1 us (4%)
    all_to_all x1, waiting for transfers between devices, per_device(): lax.all_to_all(back_keys, 'ctx', split_axis=0, concat_axis=0, tiled=True)  112 us
    all_to_all x1, waiting for transfers between devices, per_device(): lax.all_to_all(back_values, 'ctx', split_axis=0, concat_axis=0, tiled=True)  108 us
    all_to_all x1, waiting for transfers between devices, per_device(): lax.all_to_all(key_send, 'ctx', split_axis=0, concat_axis=0, tiled=True)  50.1 us
    all_to_all x1, waiting for transfers between devices, per_device(): lax.all_to_all(value_send, 'ctx', split_axis=0, concat_axis=0, tiled=True)  40 us
    unnamed x36, local copies, waits for them, and re-layouts  34.5 us
    dot_general x3, matrix products, tile_grads(): jnp.einsum('acgjb,jbcd->acgd', weights_low, value_tiles, preferred_elemen...  25.1 us
    dot_general x3, matrix products, tile_grads(): jnp.einsum('acgd,jbcd->acgjb', grad_tile, value_tiles, preferred_element_...  16.9 us
    dot_general x3, matrix products, tile_grads(): jnp.einsum('acgjb,jbcd->acgd', score_grad, key_tiles, preferred_element_t...  12 us
  transfers between devices with their start and end apart: 7, of which 6 were waited for; matrix products, arithmetic and copies ran while one was open for 12% of the time, Pallas kernels for 0%

commit v1 on v0

v1 whole, which is shorter than its diff:
```python
import functools

import jax
import jax.numpy as jnp
from jax import lax
from jax.experimental import pallas as pl
from jax.experimental.pallas import tpu as pltpu
from jax.sharding import PartitionSpec as P

HEAD = 128
BLK = 512
SIDE = 4
ROW = 6
LINE = SIDE * ROW
SCALE = 1.0 / HEAD**0.5
LOG2E = 1.4426950408889634
BIG = 3.0e38
MESH = pl.DeviceIdType.MESH
F32 = jnp.float32
LOW = jnp.bfloat16
VMEM_LIMIT = 56 * 2**20


def place():
    index = lax.axis_index("ctx")
    x, y, c = index // 8, (index // 2) % 4, index % 2
    return x, y, c, lax.axis_index("kvh")


def lines(x, y, c):
    return x * (1 - c) + y * c, y * (1 - c) + x * c


def on_first(x, y, c, z, o):
    xx = (x + o * (1 - c)) % SIDE
    yy = (y + o * c) % SIDE
    return (xx * 8 + yy * 2 + c, z)


def on_second(x, y, c, z, o):
    xx = (x + o * c) % SIDE
    yy = (y + o * (1 - c)) % SIDE
    return (xx * 8 + yy * 2 + c, z)


def layout(cap):
    at = {}
    at["send"] = 0
    at["own"] = at["send"] + 3 * cap
    at["own_far"] = at["own"] + 6
    at["sib"] = at["own_far"] + 6
    at["sib_far"] = at["sib"] + 6
    at["pack"] = at["sib_far"] + 6
    at["acc"] = at["pack"] + 2 * 3 * cap
    at["attend"] = at["acc"] + 5 * LINE
    at["size"] = at["attend"] + 12
    return at


def plan_kernel(cap, where, picked, plan, mark, part_of):
    at = layout(cap)
    index = where[0]
    x, y, c = index // 8, (index // 2) % 4, index % 2
    a, b = lines(x, y, c)
    my_chip = x * 4 + y

    def second_of(block):
        return ((block // ROW) % 4) * (1 - c) + (block // LINE) * c

    def slot24(block):
        first = (block // LINE) * (1 - c) + ((block // ROW) % 4) * c
        return first * ROW + block % ROW

    def fill(start, count, value):
        def body(k, _):
            plan[start + k] = value
            return 0

        lax.fori_loop(0, count, body, 0, unroll=6)

    fill(at["send"], 3 * cap, 0)
    fill(at["pack"], 6 * cap, 12)

    def clear(k, _):
        mark[k] = 0
        part_of[2 * k] = 12
        part_of[2 * k + 1] = 12
        return 0

    lax.fori_loop(0, 7 * LINE, clear, 0, unroll=8)

    for o in (1, 2, 3):
        other = (b + o) % 4
        chip = (x * 4 + other) * (1 - c) + (other * 4 + y) * c

        def see(k, _):
            block = picked[chip * 12 + k]

            @pl.when(second_of(block) == b)
            def _():
                mark[(3 + o) * LINE + slot24(block)] = 1

            return 0

        lax.fori_loop(0, 12, see, 0, unroll=4)

        def number(t, count):
            hit = mark[(3 + o) * LINE + t]

            @pl.when(hit == 1)
            def _():
                plan[at["send"] + (o - 1) * cap + count] = t

            plan[at["acc"] + 5 * t + o - 1] = lax.select(
                hit == 1, (o - 1) * cap + count, 3 * cap
            )
            return count + hit

        lax.fori_loop(0, LINE, number, 0, unroll=4)

    def want(k, _):
        core = 1 - k // 6
        pick = 5 - k % 6
        owner = my_chip * 2 + core
        block = picked[owner * 6 + pick]
        o = (second_of(block) - b + 4) % 4
        t = o * LINE + slot24(block)
        mark[t] = 1

        @pl.when(block // 3 != owner)
        def _():
            part_of[2 * t + lax.select(core == c, 0, 1)] = pick + lax.select(core == c, 0, 6)

        return 0

    lax.fori_loop(0, 12, want, 0, unroll=4)

    def home(t, _):
        plan[at["acc"] + 5 * t + 3] = part_of[2 * t]
        plan[at["acc"] + 5 * t + 4] = part_of[2 * t + 1]
        return 0

    lax.fori_loop(0, LINE, home, 0, unroll=4)
    for o in (1, 2, 3):

        def number(t, count):
            hit = mark[o * LINE + t]
            mark[o * LINE + t] = count

            @pl.when(hit == 1)
            def _():
                start = at["pack"] + 2 * ((o - 1) * cap + count)
                plan[start] = part_of[2 * (o * LINE + t)]
                plan[start + 1] = part_of[2 * (o * LINE + t) + 1]

            return count + hit

        lax.fori_loop(0, LINE, number, 0, unroll=4)

    for name, core in (("own", c), ("sib", 1 - c)):

        def find(k, _):
            block = picked[(my_chip * 2 + core) * 6 + k]
            o = (second_of(block) - b + 4) % 4
            t = slot24(block)
            plan[at[name] + k] = t
            plan[at[name + "_far"] + k] = lax.select(
                o == 0, -1, (lax.max(o, 1) - 1) * cap + mark[o * LINE + t]
            )
            return 0

        lax.fori_loop(0, 6, find, 0, unroll=2)

    def target(k, _):
        block = picked[index * 6 + k]
        query = index * 3 + k // 2

        def back(s, best):
            other = 5 - s
            return lax.select(picked[index * 6 + other] == block, other, best)

        first = lax.fori_loop(0, 6, back, k, unroll=6)
        plan[at["attend"] + k] = lax.select(block // 3 == index, block % 3, 3 + first)
        plan[at["attend"] + 6 + k] = lax.select(block == query, 0, 1)
        return 0

    lax.fori_loop(0, 6, target, 0)


def make_plan(cap, picked):
    where = lax.axis_index("ctx").reshape(1).astype(jnp.int32)
    smem = pl.BlockSpec(memory_space=pltpu.SMEM)
    return pl.pallas_call(
        functools.partial(plan_kernel, cap),
        out_shape=jax.ShapeDtypeStruct((layout(cap)["size"],), jnp.int32),
        in_specs=[smem, smem],
        out_specs=smem,
        scratch_shapes=[pltpu.SMEM((7 * LINE,), jnp.int32), pltpu.SMEM((14 * LINE,), jnp.int32)],
        name="plan",
    )(where, picked.reshape(-1))


def remote(src, dst, sends, recvs, k, device):
    return pltpu.make_async_remote_copy(
        src_ref=src,
        dst_ref=dst,
        send_sem=sends.at[k],
        recv_sem=recvs.at[k],
        device_id=device,
        device_id_type=MESH,
    )


def greet(devices):
    barrier = pltpu.get_barrier_semaphore()
    for device in devices:
        pl.semaphore_signal(barrier, inc=1, device_id=device, device_id_type=MESH)
    pl.semaphore_wait(barrier, len(devices))


def fetch_kernel(cap, plan, keys, values, out, pair, near, far, packed, give, take, sends, recvs):
    at = layout(cap)
    x, y, c, z = place()
    a, b = lines(x, y, c)
    sibling = (x * 8 + y * 2 + 1 - c, z)
    up, down = on_first(x, y, c, z, 1), on_first(x, y, c, z, 3)
    greet([sibling, up, down] + [on_second(x, y, c, z, o) for o in (1, 2, 3)])

    for t in range(3):
        pair[0, t] = keys[t * BLK : (t + 1) * BLK]
        pair[1, t] = values[t * BLK : (t + 1) * BLK]
    mine = near.at[pl.ds(a * ROW + c * 3, 3)]
    theirs = near.at[pl.ds(a * ROW + (1 - c) * 3, 3)]
    swap = remote(pair.at[1 - c], near.at[pl.ds(b * ROW + c * 3, 3)], sends, recvs, 0, sibling)
    swap.start()
    for t in range(3):
        near[a * ROW + c * 3 + t] = pair[c, t]
    copies = [
        remote(mine, mine, sends, recvs, 1, up),
        remote(mine, mine, sends, recvs, 2, down),
    ]
    copies[0].start()
    copies[1].start()
    swap.wait_recv()
    copies += [
        remote(theirs, theirs, sends, recvs, 3, up),
        remote(theirs, theirs, sends, recvs, 4, down),
    ]
    copies[3].start()
    copies[2].start()
    copies[0].wait_recv()
    below = near.at[pl.ds(((a + 3) % 4) * ROW + c * 3, 3)]
    copies.append(remote(below, below, sends, recvs, 5, up))
    copies[4].start()
    copies[3].wait_recv()
    above = near.at[pl.ds(((a + 1) % 4) * ROW + (1 - c) * 3, 3)]
    copies.append(remote(above, above, sends, recvs, 6, down))
    copies[5].start()
    for k in (1, 2, 4, 5):
        copies[k].wait_recv()

    passes = []
    for o in (2, 1, 3):

        def pack(s, _):
            packed[(o - 1) * cap + s] = near[plan[at["send"] + (o - 1) * cap + s]]
            return 0

        lax.fori_loop(0, cap, pack, 0)
        copy = remote(
            packed.at[pl.ds((o - 1) * cap, cap)],
            far.at[pl.ds((3 - o) * cap, cap)],
            sends,
            recvs,
            6 + o,
            on_second(x, y, c, z, o),
        )
        copy.start()
        passes.append(copy)
    for copy in passes:
        copy.wait_recv()

    def pick(name, k):
        from_far = plan[at[name + "_far"] + k]
        return jnp.where(
            from_far >= 0, far[lax.max(from_far, 0)], near[plan[at[name] + k]]
        )

    def give_one(k, _):
        give[k] = pick("sib", k)
        return 0

    lax.fori_loop(0, 6, give_one, 0)
    last = remote(give, take, sends, recvs, 10, sibling)
    last.start()

    def own_one(k, _):
        out[c, k] = pick("own", k)
        return 0

    lax.fori_loop(0, 6, own_one, 0)
    last.wait_recv()
    for k in range(6):
        out[1 - c, k] = take[k]
    for copy in [swap] + copies + passes + [last]:
        copy.wait_send()


def fetch(cap, plan, keys, values):
    vmem = pl.BlockSpec(memory_space=pltpu.VMEM)
    tile = (BLK, HEAD)
    return pl.pallas_call(
        functools.partial(fetch_kernel, cap),
        out_shape=jax.ShapeDtypeStruct((2, 6) + tile, LOW),
        in_specs=[pl.BlockSpec(memory_space=pltpu.SMEM), vmem, vmem],
        out_specs=vmem,
        scratch_shapes=[
            pltpu.VMEM((2, 3) + tile, LOW),
            pltpu.VMEM((LINE,) + tile, LOW),
            pltpu.VMEM((3 * cap,) + tile, LOW),
            pltpu.VMEM((3 * cap,) + tile, LOW),
            pltpu.VMEM((6,) + tile, LOW),
            pltpu.VMEM((6,) + tile, LOW),
            pltpu.SemaphoreType.DMA((11,)),
            pltpu.SemaphoreType.DMA((11,)),
        ],
        compiler_params=pltpu.CompilerParams(
            collective_id=0, has_side_effects=True, vmem_limit_bytes=VMEM_LIMIT
        ),
        name="fetch",
    )(plan, keys, values)


def dot(left, right, left_dim, right_dim):
    return lax.dot_general(
        left, right, (((left_dim,), (right_dim,)), ((), ())), preferred_element_type=F32
    )


def head_step(query, grad, keys, values, live, tile):
    weights_low = [[], [], []]
    score_grads = [[], [], []]
    query_grads = []
    for r in range(BLK // tile):
        rows = slice(r * tile, (r + 1) * tile)
        seen = (r + 1) * tile
        ks = [keys[0][:seen], keys[1], keys[2]]
        vs = [values[0][:seen], values[1], values[2]]
        scores = [dot(k, query[rows], 1, 1) for k in ks]
        key_at = lax.broadcasted_iota(jnp.int32, (tile, tile), 0)
        row_at = lax.broadcasted_iota(jnp.int32, (tile, tile), 1)
        corner = jnp.where(key_at <= row_at, scores[0][seen - tile :], -BIG)
        scores[0] = corner if r == 0 else jnp.concatenate([scores[0][: seen - tile], corner], 0)
        weight_grads = [dot(v, grad[rows], 1, 1) for v in vs]
        tops = [jnp.max(s, axis=0, keepdims=True) for s in scores]
        top = tops[0]
        for j in (1, 2):
            top = jnp.maximum(top, jnp.where(live[j], tops[j], -BIG))
        top = top * (SCALE * LOG2E)
        shifts = [top] + [jnp.where(live[j], top, BIG) for j in (1, 2)]
        powers = [jnp.exp2(s * (SCALE * LOG2E) - h) for s, h in zip(scores, shifts)]
        total = sum(jnp.sum(p, axis=0, keepdims=True) for p in powers)
        mixed = sum(jnp.sum(p * w, axis=0, keepdims=True) for p, w in zip(powers, weight_grads))
        inverse = 1.0 / total
        delta = mixed * inverse
        weights = [p * inverse for p in powers]
        grads = [(p * (w - delta)).astype(LOW) for p, w in zip(weights, weight_grads)]
        query_grad = sum(dot(d, k, 0, 0) for d, k in zip(grads, ks))
        query_grads.append((query_grad * SCALE).astype(LOW))
        blank = jnp.zeros((BLK - seen, tile), LOW)
        for j in range(3):
            low = weights[j].astype(LOW)
            pad = j == 0 and seen < BLK
            weights_low[j].append(jnp.concatenate([low, blank], 0) if pad else low)
            score_grads[j].append(jnp.concatenate([grads[j], blank], 0) if pad else grads[j])
    key_grads = [dot(jnp.concatenate(d, 1), query, 1, 0) for d in score_grads]
    value_grads = [dot(jnp.concatenate(w, 1), grad, 1, 0) for w in weights_low]
    return jnp.concatenate(query_grads, 0), key_grads, value_grads


def attend_kernel(start, plan, query, grad, key0, value0, pick1, pick2, query_grad, own, picks, acc, sums):
    i = pl.program_id(0)

    @pl.when(i == 0)
    def _():
        sums[...] = jnp.zeros_like(sums)

    acc[...] = jnp.zeros_like(acc)
    live = (True, plan[start + 6 + 2 * i] == 1, plan[start + 7 + 2 * i] == 1)

    def body(h, _):
        columns = pl.ds(pl.multiple_of(h * HEAD, HEAD), HEAD)
        keys = [key0[...], pick1[0, 0], pick2[0, 0]]
        values = [value0[...], pick1[1, 0], pick2[1, 0]]
        part, key_grads, value_grads = head_step(
            query[:, columns], grad[:, columns], keys, values, live, 256
        )
        query_grad[:, columns] = part
        for j in range(3):
            acc[j, 0] += key_grads[j]
            acc[j, 1] += value_grads[j]
        return 0

    lax.fori_loop(0, query.shape[1] // HEAD, body, 0)
    for j in range(3):
        to = i if j == 0 else plan[start + 2 * i + j - 1]
        sums[to, 0] += acc[j, 0] * SCALE
        sums[to, 1] += acc[j, 1]

    @pl.when(i == 2)
    def _():
        for s in range(2):
            for t in range(3):
                own[s, t] = sums[t, s]
            for t in range(6):
                picks[s, t] = sums[3 + t, s].astype(LOW)


def attend(cap, plan, queries, out_grad, keys, values, fetched):
    start = layout(cap)["attend"]
    tile = (BLK, HEAD)
    rows = pl.BlockSpec((BLK, queries.shape[1]), lambda i, plan: (i, 0))
    own_rows = pl.BlockSpec(tile, lambda i, plan: (i, 0))
    grid_spec = pltpu.PrefetchScalarGridSpec(
        num_scalar_prefetch=1,
        grid=(3,),
        in_specs=[
            rows,
            rows,
            own_rows,
            own_rows,
            pl.BlockSpec((2, 1) + tile, lambda i, plan: (0, 2 * i, 0, 0)),
            pl.BlockSpec((2, 1) + tile, lambda i, plan: (0, 2 * i + 1, 0, 0)),
        ],
        out_specs=[
            rows,
            pl.BlockSpec((2, 3) + tile, lambda i, plan: (0, 0, 0, 0)),
            pl.BlockSpec((2, 6) + tile, lambda i, plan: (0, 0, 0, 0)),
        ],
        scratch_shapes=[pltpu.VMEM((3, 2) + tile, F32), pltpu.VMEM((9, 2) + tile, F32)],
    )
    return pl.pallas_call(
        functools.partial(attend_kernel, start),
        grid_spec=grid_spec,
        out_shape=[
            jax.ShapeDtypeStruct(queries.shape, LOW),
            jax.ShapeDtypeStruct((2, 3) + tile, F32),
            jax.ShapeDtypeStruct((2, 6) + tile, LOW),
        ],
        compiler_params=pltpu.CompilerParams(vmem_limit_bytes=VMEM_LIMIT),
        name="attend",
    )(plan, queries, out_grad, keys, values, fetched, fetched)


def give_back_kernel(
    cap, plan, query_grad, own, picks, query_out, key_out, value_out,
    parts, own_far, packed, came, to_first, from_first, home, done, landed,
    sends, recvs, query_sems, query_recvs, final_sends, final_recvs, local_sems,
):
    at = layout(cap)
    x, y, c, z = place()
    a, b = lines(x, y, c)
    sibling = (x * 8 + y * 2 + 1 - c, z)
    here = x * 8 + y * 2
    firsts = {o: on_first(x, y, c, z, o) for o in (1, 2, 3)}
    seconds = {o: on_second(x, y, c, z, o) for o in (1, 2, 3)}
    depth = {(k, o): (here + k, (z + o) % SIDE) for k in (0, 1) for o in (1, 2, 3)}
    greet(
        [sibling] + list(firsts.values()) + list(seconds.values()) + list(depth.values())
    )
    rows = query_out.shape[0]
    width = query_grad.shape[1]

    swap = remote(picks.at[1 - c], parts.at[pl.ds(6, 6)], sends, recvs, 0, sibling)
    swap.start()
    swap_own = remote(own.at[1 - c], own_far, sends, recvs, 1, sibling)
    swap_own.start()
    query_copies = []
    for o in (2, 1, 3):
        copy = remote(
            query_grad.at[pl.ds(((z + o) % SIDE) * rows, rows)],
            query_out.at[:, pl.ds(pl.multiple_of(z * width, HEAD), width)],
            query_sems,
            query_recvs,
            o - 1,
            (here + c, (z + o) % SIDE),
        )
        copy.start()
        query_copies.append(copy)
    stay = pltpu.make_async_copy(
        query_grad.at[pl.ds(z * rows, rows)],
        query_out.at[:, pl.ds(pl.multiple_of(z * width, HEAD), width)],
        local_sems.at[0],
    )
    stay.start()

    for t in range(6):
        parts[t] = picks[c, t]
    parts[12] = jnp.zeros((BLK, HEAD), LOW)
    came[3 * cap] = jnp.zeros((BLK, HEAD), LOW)
    swap.wait_recv()

    passes = []
    for o in (2, 1, 3):

        def pack(s, _):
            start = at["pack"] + 2 * ((o - 1) * cap + s)
            total = parts[plan[start]].astype(F32) + parts[plan[start + 1]].astype(F32)
            packed[(o - 1) * cap + s] = total.astype(LOW)
            return 0

        lax.fori_loop(0, cap, pack, 0)
        copy = remote(
            packed.at[pl.ds((o - 1) * cap, cap)],
            came.at[pl.ds((3 - o) * cap, cap)],
            sends,
            recvs,
            1 + o,
            seconds[o],
        )
        copy.start()
        passes.append(copy)
    for copy in passes:
        copy.wait_recv()

    def line_sum(t):
        start = at["acc"] + 5 * t
        total = came[plan[start]].astype(F32)
        for k in (1, 2):
            total += came[plan[start + k]].astype(F32)
        for k in (3, 4):
            total += parts[plan[start + k]].astype(F32)
        return total

    homeward = []
    for o in (2, 1, 3):
        line = (a + o) % SIDE

        def one(t, _):
            to_first[(o - 1) * ROW + t] = line_sum(line * ROW + t).astype(LOW)
            return 0

        lax.fori_loop(0, ROW, one, 0)
        copy = remote(
            to_first.at[pl.ds((o - 1) * ROW, ROW)],
            from_first.at[pl.ds((3 - o) * ROW, ROW)],
            sends,
            recvs,
            4 + o,
            firsts[o],
        )
        copy.start()
        homeward.append(copy)
    swap_own.wait_recv()

    def mine(t, _):
        home[c * 3 + t] = line_sum(a * ROW + c * 3 + t) + own[c, t]
        home[(1 - c) * 3 + t] = line_sum(a * ROW + (1 - c) * 3 + t) + own_far[t]
        return 0

    lax.fori_loop(0, 3, mine, 0)
    for copy in homeward:
        copy.wait_recv()

    finals = []
    columns = pl.ds(pl.multiple_of(z * HEAD, HEAD), HEAD)
    for k in (0, 1):

        def finish(t, _):
            total = home[k * 3 + t]
            for o in range(3):
                total += from_first[o * ROW + k * 3 + t].astype(F32)
            done[k, pl.ds(pl.multiple_of(t * BLK, BLK), BLK)] = total.astype(LOW)
            return 0

        lax.fori_loop(0, 3, finish, 0)
        for o in (2, 1, 3):
            copy = remote(
                done.at[k, pl.ds(((z + o) % SIDE) * rows, rows)],
                landed.at[c, :, columns],
                final_sends.at[k],
                final_recvs.at[c],
                o,
                depth[k, o],
            )
            copy.start()
            finals.append(copy)
    cross = remote(
        done.at[1 - c, pl.ds(z * rows, rows)],
        landed.at[c, :, columns],
        final_sends.at[1 - c],
        final_recvs.at[c],
        0,
        sibling,
    )
    cross.start()
    keep = pltpu.make_async_copy(
        done.at[c, pl.ds(z * rows, rows)], landed.at[c, :, columns], local_sems.at[1]
    )
    keep.start()
    keep.wait()
    for role in (0, 1):
        for o in (1, 2, 3):
            remote(
                done.at[0, pl.ds(0, rows)],
                landed.at[role, :, pl.ds(0, HEAD)],
                final_sends.at[0],
                final_recvs.at[role],
                o,
                sibling,
            ).wait_recv()
    remote(
        done.at[0, pl.ds(0, rows)],
        landed.at[1 - c, :, columns],
        final_sends.at[0],
        final_recvs.at[1 - c],
        0,
        sibling,
    ).wait_recv()
    key_out[...] = landed[0]
    value_out[...] = landed[1]
    for copy in query_copies:
        copy.wait()
    stay.wait()
    for copy in [swap, swap_own] + passes + homeward + finals + [cross]:
        copy.wait_send()


def give_back(cap, plan, query_grad, own, picks):
    vmem = pl.BlockSpec(memory_space=pltpu.VMEM)
    anywhere = pl.BlockSpec(memory_space=pl.ANY)
    tile = (BLK, HEAD)
    rows = query_grad.shape[0] // SIDE
    dma = pltpu.SemaphoreType.DMA
    return pl.pallas_call(
        functools.partial(give_back_kernel, cap),
        out_shape=[
            jax.ShapeDtypeStruct((rows, SIDE * query_grad.shape[1]), LOW),
            jax.ShapeDtypeStruct((rows, SIDE * HEAD), LOW),
            jax.ShapeDtypeStruct((rows, SIDE * HEAD), LOW),
        ],
        in_specs=[pl.BlockSpec(memory_space=pltpu.SMEM), anywhere, vmem, vmem],
        out_specs=[anywhere, vmem, vmem],
        scratch_shapes=[
            pltpu.VMEM((13,) + tile, LOW),
            pltpu.VMEM((3,) + tile, F32),
            pltpu.VMEM((3 * cap,) + tile, LOW),
            pltpu.VMEM((3 * cap + 1,) + tile, LOW),
            pltpu.VMEM((3 * ROW,) + tile, LOW),
            pltpu.VMEM((3 * ROW,) + tile, LOW),
            pltpu.VMEM((ROW,) + tile, F32),
            pltpu.VMEM((2, 3 * BLK, HEAD), LOW),
            pltpu.VMEM((2, rows, SIDE * HEAD), LOW),
            dma((8,)),
            dma((8,)),
            dma((3,)),
            dma((3,)),
            dma((2, 4)),
            dma((2, 4)),
            dma((2,)),
        ],
        compiler_params=pltpu.CompilerParams(
            collective_id=1, has_side_effects=True, vmem_limit_bytes=VMEM_LIMIT
        ),
        name="give_back",
    )(plan, query_grad, own, picks)


def per_device(queries, key_rows, value_rows, out_grad, picked):
    cap = 12
    plan = make_plan(cap, picked)
    fetched = fetch(cap, plan, key_rows, value_rows)
    query_grad, own, picks = attend(
        cap, plan, queries, out_grad, key_rows, value_rows, fetched
    )
    return tuple(give_back(cap, plan, query_grad, own, picks))


def solution(mesh):
    return jax.shard_map(
        per_device,
        mesh=mesh,
        in_specs=(P("ctx", "kvh"), P("ctx", "kvh"), P("ctx", "kvh"), P("ctx", "kvh"), P()),
        out_specs=(P(("ctx", "kvh"), None), P(("ctx", "kvh"), None), P(("ctx", "kvh"), None)),
        check_vma=False,
    )
```

time: 588 us -> 199 us (0.34)
  the two profiles are of different devices: /device:TPU:8 before, /device:TPU:1 now
where the time goes in v1:
time: 199 us
  Pallas kernels  192 us (96%)
  local copies, waits for them, and re-layouts  5.78 us (3%)
    pallas_call x1, Pallas kernels, give_back(): pl.pallas_call(functools.partial(give_back_kernel, cap), out_shape=[jax.S...  77.6 us
    pallas_call x1, Pallas kernels, fetch(): pl.pallas_call(functools.partial(fetch_kernel, cap), out_shape=jax.ShapeD...  65 us
    pallas_call x1, Pallas kernels, attend(): pl.pallas_call(functools.partial(attend_kernel, start), grid_spec=grid_sp...  45.2 us
    unnamed x8, local copies, waits for them, and re-layouts  5.08 us
    pallas_call x1, Pallas kernels, make_plan(): pl.pallas_call(functools.partial(plan_kernel, cap), out_shape=jax.ShapeDt...  4.27 us

profile of v1, /device:TPU:1, one launch (start us, length us, event | category | flops | bytes accessed | tf_op | source)
XLA Modules:
  0.0 198.5 jit_solution(16492245796959609085)
XLA Ops:
  0.6 0.8 copy.8
  1.4 0.7 reshape.13.picked
  2.1 4.3 %plan.1 = s32[264]{0:T(512)} custom-call(s32[1]{0:T(128)} %bitcast.where, s32[192]{0:T(256)} %reshape.13.picked), custom_call_target="tpu_custom_call" | custom-call | tf_op jit(solution)/shard_map/plan/pallas_call | solution.py:193
  6.4 65.0 %fetch.1.pick1.pick2 = bf16[2,6,512,128]{3,2,1,0:T(8,128)(2,1)} custom-call(s32[264]{0:T(512)} %plan.1, bf16[1536,128]{1,0:T(8,128)(2,1)} %key0.1, bf16[1536,128]{1,0:T(8,128)(2,1)} %value0.1), custom_call_target="tpu_custom_call" | custom-call | tf_op jit(solution)/shard_map/fetch/pallas_call | solution.py:312
  71.4 45.2 %attend.1 = (bf16[1536,512]{1,0:T(8,128)(2,1)}, f32[2,3,512,128]{3,2,1,0:T(8,128)}, bf16[2,6,512,128]{3,2,1,0:T(8,128)(2,1)}) custom-call(s32[264]{0:T(512)} %plan.1, bf16[1536,512]{1,0:T(8,128)(2,1)} %query.1, bf16[1536,512]{1,0:T(8,128)(2,1)} %grad.1, bf16[1536,128]{1,0:T(8,128)(2,1)} %key0.1, bf16[1536,128]{1,0:T(8,128)(2,1)} %value0.1, ...), custom_call_target="tpu_custom_call" | custom-call | tf_op jit(solution)/shard_map/attend/pallas_call | solution.py:442
  116.6 77.6 %give_back.1 = (bf16[384,2048]{1,0:T(8,128)(2,1)}, bf16[384,512]{1,0:T(8,128)(2,1)}, bf16[384,512]{1,0:T(8,128)(2,1)}) custom-call(s32[264]{0:T(512)} %plan.1, bf16[1536,512]{1,0:T(8,128)(2,1)} %get-tuple-element.6.query_grad, f32[2,3,512,128]{3,2,1,0:T(8,128)} %get-tuple-element.7.own, bf16[2,6,512,128]{3,2,1,0:T(8,128)(2,1)} %get-tuple-element.8.picks), custom_call_target="tpu_custom_call" | custom-call | tf_op jit(solution)/shard_map/give_back/pallas_call | solution.py:635
  194.2 0.0 copy-start.1
  194.2 0.0 copy-start
  194.2 2.8 %copy.12 = bf16[384,2048]{1,0:T(8,128)(2,1)} copy(bf16[384,2048]{1,0:T(8,128)(2,1)} %get-tuple-element.12) | data formatting | bytes 3145728
  197.0 0.0 copy-done.1
  197.0 0.7 copy.13
  197.8 0.0 copy-done
  197.8 0.7 copy.14
Async XLA Ops:
  194.2 2.8 %copy-start.1 = (bf16[384,512]{1,0:T(8,128)(2,1)S(1)}, bf16[384,512]{1,0:T(8,128)(2,1)}, u32[]{:S(2)}) copy-start(bf16[384,512]{1,0:T(8,128)(2,1)} %get-tuple-element.13) | copy-start | bytes 1179652
  194.2 3.6 %copy-start = (bf16[384,512]{1,0:T(8,128)(2,1)S(1)}, bf16[384,512]{1,0:T(8,128)(2,1)}, u32[]{:S(2)}) copy-start(bf16[384,512]{1,0:T(8,128)(2,1)} %get-tuple-element.14) | copy-start | bytes 1179652

commit v2 on v0

v2 whole, which is shorter than its diff:
```python
import functools

import jax
import jax.numpy as jnp
from jax import lax
from jax.experimental import pallas as pl
from jax.experimental.pallas import tpu as pltpu
from jax.sharding import PartitionSpec as P

HEAD = 128
BLK = 512
SIDE = 4
ROW = 6
LINE = SIDE * ROW
SCALE = 1.0 / HEAD**0.5
LOG2E = 1.4426950408889634
BIG = 3.0e38
MESH = pl.DeviceIdType.MESH
F32 = jnp.float32
LOW = jnp.bfloat16
VMEM_LIMIT = 56 * 2**20


def place():
    index = lax.axis_index("ctx")
    x, y, c = index // 8, (index // 2) % 4, index % 2
    return x, y, c, lax.axis_index("kvh")


def lines(x, y, c):
    return x * (1 - c) + y * c, y * (1 - c) + x * c


def on_first(x, y, c, z, o):
    xx = (x + o * (1 - c)) % SIDE
    yy = (y + o * c) % SIDE
    return (xx * 8 + yy * 2 + c, z)


def on_second(x, y, c, z, o):
    xx = (x + o * c) % SIDE
    yy = (y + o * (1 - c)) % SIDE
    return (xx * 8 + yy * 2 + c, z)


def remote(src, dst, sends, recvs, k, device):
    return pltpu.make_async_remote_copy(
        src_ref=src,
        dst_ref=dst,
        send_sem=sends.at[k],
        recv_sem=recvs.at[k],
        device_id=device,
        device_id_type=MESH,
    )


def greet(devices):
    barrier = pltpu.get_barrier_semaphore()
    for device in devices:
        pl.semaphore_signal(barrier, inc=1, device_id=device, device_id_type=MESH)
    pl.semaphore_wait(barrier, len(devices))


def dot(left, right, left_dim, right_dim):
    return lax.dot_general(
        left, right, (((left_dim,), (right_dim,)), ((), ())), preferred_element_type=F32
    )


def head_step(query, grad, keys, values, live, tile):
    weights_low = [[], [], []]
    score_grads = [[], [], []]
    query_grads = []
    for r in range(BLK // tile):
        rows = slice(r * tile, (r + 1) * tile)
        seen = (r + 1) * tile
        ks = [keys[0][:seen], keys[1], keys[2]]
        vs = [values[0][:seen], values[1], values[2]]
        scores = [dot(k, query[rows], 1, 1) for k in ks]
        key_at = lax.broadcasted_iota(jnp.int32, (tile, tile), 0)
        row_at = lax.broadcasted_iota(jnp.int32, (tile, tile), 1)
        corner = jnp.where(key_at <= row_at, scores[0][seen - tile :], -BIG)
        scores[0] = corner if r == 0 else jnp.concatenate([scores[0][: seen - tile], corner], 0)
        weight_grads = [dot(v, grad[rows], 1, 1) for v in vs]
        tops = [jnp.max(s, axis=0, keepdims=True) for s in scores]
        top = tops[0]
        for j in (1, 2):
            top = jnp.maximum(top, jnp.where(live[j], tops[j], -BIG))
        top = top * (SCALE * LOG2E)
        shifts = [top] + [jnp.where(live[j], top, BIG) for j in (1, 2)]
        powers = [jnp.exp2(s * (SCALE * LOG2E) - h) for s, h in zip(scores, shifts)]
        total = sum(jnp.sum(p, axis=0, keepdims=True) for p in powers)
        mixed = sum(jnp.sum(p * w, axis=0, keepdims=True) for p, w in zip(powers, weight_grads))
        inverse = 1.0 / total
        delta = mixed * inverse
        weights = [p * inverse for p in powers]
        grads = [(p * (w - delta)).astype(LOW) for p, w in zip(weights, weight_grads)]
        query_grad = sum(dot(d, k, 0, 0) for d, k in zip(grads, ks))
        query_grads.append((query_grad * SCALE).astype(LOW))
        blank = jnp.zeros((BLK - seen, tile), LOW)
        for j in range(3):
            low = weights[j].astype(LOW)
            pad = j == 0 and seen < BLK
            weights_low[j].append(jnp.concatenate([low, blank], 0) if pad else low)
            score_grads[j].append(jnp.concatenate([grads[j], blank], 0) if pad else grads[j])
    key_grads = [dot(jnp.concatenate(d, 1), query, 1, 0) for d in score_grads]
    value_grads = [dot(jnp.concatenate(w, 1), grad, 1, 0) for w in weights_low]
    return jnp.concatenate(query_grads, 0), key_grads, value_grads


def second_of(block, c):
    return ((block // ROW) % 4) * (1 - c) + (block // LINE) * c


def near_at(block, c):
    first = (block // LINE) * (1 - c) + ((block // ROW) % 4) * c
    return first * ROW + block % ROW


def kernel(
    picked, queries, keys, values, out_grad, query_out, key_out, value_out,
    query_v, grad_v, query_grad, pair, near, give, chosen, acc, own, own_far, other_part,
    sums, to_first, from_first, home, done, landed, at_home,
    sends, recvs, query_sems, query_recvs, final_sends, final_recvs, local_sems,
    *rounds,
):
    packed, far, parts, merged, came = (rounds[3 * k : 3 * k + 3] for k in range(5))
    x, y, c, z = place()
    a, b = lines(x, y, c)
    index = x * 8 + y * 2 + c
    chip = x * 4 + y
    here = x * 8 + y * 2
    sibling = (here + 1 - c, z)
    firsts = {o: on_first(x, y, c, z, o) for o in (1, 2, 3)}
    seconds = {o: on_second(x, y, c, z, o) for o in (1, 2, 3)}
    depth = {(k, o): (here + k, (z + o) % SIDE) for k in (0, 1) for o in (1, 2, 3)}
    up, down = firsts[1], firsts[3]

    loads = [
        pltpu.make_async_copy(queries, query_v, local_sems.at[2]),
        pltpu.make_async_copy(out_grad, grad_v, local_sems.at[3]),
    ]
    for load in loads:
        load.start()
    for t in range(3):
        pair[0, t] = keys[t * BLK : (t + 1) * BLK]
        pair[1, t] = values[t * BLK : (t + 1) * BLK]
    for t in range(3):
        near[a * ROW + c * 3 + t] = pair[c, t]
    greet([sibling, up, down, seconds[1], seconds[3]] + list(depth.values()))

    mine = near.at[pl.ds(a * ROW + c * 3, 3)]
    theirs = near.at[pl.ds(a * ROW + (1 - c) * 3, 3)]
    swap = remote(pair.at[1 - c], near.at[pl.ds(b * ROW + c * 3, 3)], sends, recvs, 0, sibling)
    swap.start()
    copies = [
        remote(mine, mine, sends, recvs, 1, up),
        remote(mine, mine, sends, recvs, 2, down),
    ]
    copies[0].start()
    copies[1].start()
    swap.wait_recv()
    copies += [
        remote(theirs, theirs, sends, recvs, 3, up),
        remote(theirs, theirs, sends, recvs, 4, down),
    ]
    copies[3].start()
    copies[2].start()
    copies[0].wait_recv()
    below = near.at[pl.ds(((a + 3) % 4) * ROW + c * 3, 3)]
    copies.append(remote(below, below, sends, recvs, 5, up))
    copies[4].start()
    copies[3].wait_recv()
    above = near.at[pl.ds(((a + 1) % 4) * ROW + (1 - c) * 3, 3)]
    copies.append(remote(above, above, sends, recvs, 6, down))
    copies[5].start()

    def chip_at(o):
        other = (b + o) % SIDE
        return (x * 4 + other) * (1 - c) + (other * 4 + y) * c

    def pick_of(of_chip, r, s):
        return picked[(of_chip * ROW + (s // 2) * 3 + r) * 2 + s % 2]

    for r in range(3):
        for o in range(4):
            line_chip = chip_at(o)
            blocks = [pick_of(line_chip, r, s) for s in range(4)]
            for s in range(4):
                known = second_of(blocks[s], c) == b
                if s >= 2:
                    again = jnp.logical_or(blocks[s] == blocks[0], blocks[s] == blocks[1])
                    known = jnp.logical_and(known, jnp.logical_not(again))
                at_home[(r * 4 + o) * 4 + s] = jnp.where(known, near_at(blocks[s], c), -1)
    for k in (1, 2, 4, 5):
        copies[k].wait_recv()

    above2, below2 = seconds[1], seconds[3]

    def flow(r, m):
        place_at = pl.ds(2 * m, 2)
        target = below2 if m in (1, 4, 5) else above2
        return remote(packed[r].at[place_at], far[r].at[place_at], sends, recvs, 7 + 6 * r + m, target)

    def served(r, o, k):
        block = pick_of(chip_at(o), r, k)
        hit = second_of(block, c) == b
        return hit, near[jnp.where(hit, near_at(block, c), 0)]

    def send_round(r):
        for m, o, first in ((0, 2, 2), (1, 2, 0), (2, 1, 0), (5, 3, 2)):
            for k in range(2):
                packed[r][2 * m + k] = served(r, o, first + k)[1]
            flow(r, m).start()

    def relay_round(r):
        for m, o, first in ((3, 1, 2), (4, 3, 0)):
            flow(r, m - 3).wait_recv()
            for k in range(2):
                hit, block = served(r, o, first + k)
                packed[r][2 * m + k] = jnp.where(hit, block, far[r][2 * (m - 3) + k])
            flow(r, m).start()

    def chosen_copy(r):
        return remote(
            give.at[pl.ds(2 * r, 2)], chosen.at[pl.ds(4 * r + 2 * c, 2)], sends, recvs, 25 + r, sibling
        )

    def take_round(r):
        for m in (2, 3, 4, 5):
            flow(r, m).wait_recv()

        def pick(core, j):
            k = core * 2 + j
            block = pick_of(chip, r, k)
            o = (second_of(block, c) - b + 4) % 4
            over = jnp.logical_or(o == 1, jnp.logical_and(o == 2, k < 2))
            from_far = far[r][jnp.where(over, 8 + k, 4 + k)]
            return jnp.where(o > 0, from_far, near[near_at(block, c)])

        for j in range(2):
            give[2 * r + j] = pick(1 - c, j)
        chosen_copy(r).start()
        for j in range(2):
            chosen[4 * r + 2 * c + j] = pick(c, j)

    def part_copy(r):
        return remote(
            other_part.at[pl.ds(2 * r, 2)], parts[r].at[pl.ds(2 * c, 2)], sends, recvs, 28 + r, sibling
        )

    def give_round(r):
        for j in range(2):
            for role in range(2):
                value = acc[1 + j, role] * SCALE if role == 0 else acc[1 + j, role]
                low = value.astype(LOW)

                @pl.when(c == role)
                def _():
                    parts[r][2 * c + j] = low

                @pl.when(c != role)
                def _():
                    other_part[2 * r + j] = low

        part_copy(r).start()

    def back_flow(r, m):
        source, start, at, target = (
            (merged[r], 0, 8, above2),
            (merged[r], 2, 10, above2),
            (merged[r], 2, 2, below2),
            (merged[r], 0, 0, below2),
            (came[r], 8, 4, above2),
            (came[r], 2, 6, below2),
        )[m]
        return remote(
            source.at[pl.ds(start, 2)], came[r].at[pl.ds(at, 2)], sends, recvs, 31 + 6 * r + m, target
        )

    def back_round(r):
        part_copy(r).wait_recv()
        blocks = [pick_of(chip, r, s) for s in range(4)]
        for s in range(2):
            same = [blocks[k] == blocks[s] for k in (2, 3)]
            if s == 1:
                same = [jnp.logical_and(k, blocks[0] != blocks[1]) for k in same]
            extra = parts[r][jnp.where(same[0], 2, jnp.where(same[1], 3, 4))]
            merged[r][s] = (parts[r][s].astype(F32) + extra.astype(F32)).astype(LOW)
        for s in (2, 3):
            merged[r][s] = parts[r][s]
        for m in (0, 2, 1, 3):
            back_flow(r, m).start()

    def back_relay(r):
        for m in (0, 2):
            back_flow(r, m).wait_recv()
            back_flow(r, 4 + m // 2).start()

    send_round(0)
    blank = jnp.zeros((BLK, HEAD), LOW)
    for r in range(3):
        parts[r][4] = blank
        merged[r][4] = blank
        came[r][12] = blank
    for load in loads:
        load.wait()
    relay_round(0)
    take_round(0)
    chosen_copy(0).wait_recv()

    for r in range(3):
        if r < 2:
            send_round(r + 1)
        acc[...] = jnp.zeros_like(acc)
        rows = pl.ds(r * BLK, BLK)
        block = index * 3 + r
        live = (True, picked[2 * block] != block, picked[2 * block + 1] != block)

        def body(h, _):
            @pl.when(h == 1)
            def _():
                if r < 2:
                    relay_round(r + 1)
                if r > 0:
                    back_round(r - 1)

            @pl.when(h == 2)
            def _():
                if r > 0:
                    back_relay(r - 1)

            @pl.when(h == 3)
            def _():
                if r < 2:
                    take_round(r + 1)

            columns = pl.ds(pl.multiple_of(h * HEAD, HEAD), HEAD)
            key_tiles = [keys[rows], chosen[4 * r], chosen[4 * r + 1]]
            value_tiles = [values[rows], chosen[4 * r + 2], chosen[4 * r + 3]]
            part, key_grads, value_grads = head_step(
                query_v[rows, columns], grad_v[rows, columns], key_tiles, value_tiles, live, 256
            )
            query_grad[rows, columns] = part
            for j in range(3):
                acc[j, 0] += key_grads[j]
                acc[j, 1] += value_grads[j]
            return 0

        lax.fori_loop(0, 4, body, 0)
        own[0, r] = acc[0, 0] * SCALE
        own[1, r] = acc[0, 1]
        give_round(r)
        if r < 2:
            chosen_copy(r + 1).wait_recv()

    swap_own = remote(own.at[1 - c], own_far, sends, recvs, 49, sibling)
    swap_own.start()
    height = query_out.shape[0]
    width = query_grad.shape[1]
    query_columns = pl.ds(pl.multiple_of(z * width, HEAD), width)
    back_round(2)
    query_copies = []
    for o in (2, 1, 3):
        copy = remote(
            query_grad.at[pl.ds(((z + o) % SIDE) * height, height)],
            query_out.at[:, query_columns],
            query_sems,
            query_recvs,
            o - 1,
            (index, (z + o) % SIDE),
        )
        copy.start()
        query_copies.append(copy)
    stay = pltpu.make_async_copy(
        query_grad.at[pl.ds(z * height, height)], query_out.at[:, query_columns], local_sems.at[0]
    )
    stay.start()

    def round_sum(r, t):
        total = None
        for o in range(4):
            start = (r * 4 + o) * 4
            base = max(o - 1, 0) * 4
            spot = 4 if o == 0 else 12
            for s in (3, 2, 1, 0):
                spot = jnp.where(at_home[start + s] == t, base + s, spot)
            value = (merged[r] if o == 0 else came[r])[spot].astype(F32)
            total = value if total is None else total + value
        return total

    for r in (0, 1):
        for m in (1, 3, 4, 5):
            back_flow(r, m).wait_recv()

    def early(t, _):
        sums[t] = round_sum(0, t) + round_sum(1, t)
        return 0

    lax.fori_loop(0, LINE // 2, early, 0)
    back_relay(2)
    lax.fori_loop(LINE // 2, LINE, early, 0)
    swap_own.wait_recv()

    def add_own(t, _):
        sums[a * ROW + c * 3 + t] += own[c, t]
        sums[a * ROW + (1 - c) * 3 + t] += own_far[t]
        return 0

    lax.fori_loop(0, 3, add_own, 0)
    for m in (1, 3, 4, 5):
        back_flow(2, m).wait_recv()

    def homeward(m):
        place_at = pl.ds(3 * m, 3)
        target = down if m in (1, 2, 5) else up
        return remote(to_first.at[place_at], from_first.at[place_at], sends, recvs, 50 + m, target)

    for m, o, core in ((0, 2, 0), (2, 3, 0), (1, 2, 1), (3, 1, 1)):
        start = ((a + o) % SIDE) * ROW + core * 3

        def one(t, _):
            to_first[3 * m + t] = (sums[start + t] + round_sum(2, start + t)).astype(LOW)
            return 0

        lax.fori_loop(0, 3, one, 0)
        homeward(m).start()
    for m, o, core in ((4, 1, 0), (5, 3, 1)):
        start = ((a + o) % SIDE) * ROW + core * 3

        def ready(t, _):
            sums[start + t] += round_sum(2, start + t)
            return 0

        def one(t, _):
            to_first[3 * m + t] = (sums[start + t] + from_first[3 * (m - 4) + t].astype(F32)).astype(LOW)
            return 0

        lax.fori_loop(0, 3, ready, 0)
        homeward(m - 4).wait_recv()
        lax.fori_loop(0, 3, one, 0)
        homeward(m).start()

    def stays(t, _):
        home[t] = sums[a * ROW + t] + round_sum(2, a * ROW + t)
        return 0

    lax.fori_loop(0, ROW, stays, 0)

    finals = []
    columns = pl.ds(pl.multiple_of(z * HEAD, HEAD), HEAD)
    for k in (0, 1):
        for m in (2 + k, 4 + k):
            homeward(m).wait_recv()

        def finish(t, _):
            total = home[k * 3 + t]
            for m in (2 + k, 4 + k):
                total += from_first[3 * m + t].astype(F32)
            done[k, pl.ds(pl.multiple_of(t * BLK, BLK), BLK)] = total.astype(LOW)
            return 0

        lax.fori_loop(0, 3, finish, 0)
        for o in (2, 1, 3):
            copy = remote(
                done.at[k, pl.ds(((z + o) % SIDE) * height, height)],
                landed.at[c, :, columns],
                final_sends.at[k],
                final_recvs.at[c],
                o,
                depth[k, o],
            )
            copy.start()
            finals.append(copy)
    cross = remote(
        done.at[1 - c, pl.ds(z * height, height)],
        landed.at[c, :, columns],
        final_sends.at[1 - c],
        final_recvs.at[c],
        0,
        sibling,
    )
    cross.start()
    keep = pltpu.make_async_copy(
        done.at[c, pl.ds(z * height, height)], landed.at[c, :, columns], local_sems.at[1]
    )
    keep.start()
    keep.wait()
    for role in (0, 1):
        for o in (1, 2, 3):
            remote(
                done.at[0, pl.ds(0, height)],
                landed.at[role, :, pl.ds(0, HEAD)],
                final_sends.at[0],
                final_recvs.at[role],
                o,
                sibling,
            ).wait_recv()
    remote(
        done.at[0, pl.ds(0, height)],
        landed.at[1 - c, :, columns],
        final_sends.at[0],
        final_recvs.at[1 - c],
        0,
        sibling,
    ).wait_recv()
    key_out[...] = landed[0]
    value_out[...] = landed[1]
    for copy in query_copies:
        copy.wait()
    stay.wait()
    ends = [swap, swap_own] + copies + finals + [cross] + [homeward(m) for m in range(6)]
    for r in range(3):
        ends += [chosen_copy(r), part_copy(r)]
        ends += [flow(r, m) for m in range(6)] + [back_flow(r, m) for m in range(6)]
    for copy in ends:
        copy.wait_send()


def per_device(queries, key_rows, value_rows, out_grad, picked):
    vmem = pl.BlockSpec(memory_space=pltpu.VMEM)
    anywhere = pl.BlockSpec(memory_space=pl.ANY)
    tile = (BLK, HEAD)
    tokens, width = queries.shape
    height = tokens // SIDE
    dma = pltpu.SemaphoreType.DMA

    def blocks(count, kind=LOW):
        return pltpu.VMEM((count,) + tile, kind)

    return tuple(
        pl.pallas_call(
            kernel,
            out_shape=[
                jax.ShapeDtypeStruct((height, SIDE * width), LOW),
                jax.ShapeDtypeStruct((height, SIDE * HEAD), LOW),
                jax.ShapeDtypeStruct((height, SIDE * HEAD), LOW),
            ],
            in_specs=[pl.BlockSpec(memory_space=pltpu.SMEM), anywhere, vmem, vmem, anywhere],
            out_specs=[anywhere, vmem, vmem],
            scratch_shapes=[
                pltpu.VMEM((tokens, width), LOW),
                pltpu.VMEM((tokens, width), LOW),
                pltpu.VMEM((tokens, width), LOW),
                pltpu.VMEM((2, 3) + tile, LOW),
                blocks(LINE),
                blocks(6),
                blocks(12),
                pltpu.VMEM((3, 2) + tile, F32),
                pltpu.VMEM((2, 3) + tile, F32),
                blocks(3, F32),
                blocks(6),
                blocks(LINE, F32),
                blocks(3 * ROW),
                blocks(3 * ROW),
                blocks(ROW, F32),
                pltpu.VMEM((2, 3 * BLK, HEAD), LOW),
                pltpu.VMEM((2, height, SIDE * HEAD), LOW),
                pltpu.SMEM((48,), jnp.int32),
                dma((56,)),
                dma((56,)),
                dma((3,)),
                dma((3,)),
                dma((2, 4)),
                dma((2, 4)),
                dma((4,)),
            ]
            + [blocks(12)] * 6
            + [blocks(5)] * 6
            + [blocks(13)] * 3,
            compiler_params=pltpu.CompilerParams(
                collective_id=0, has_side_effects=True, vmem_limit_bytes=VMEM_LIMIT
            ),
            name="attend",
        )(picked.reshape(-1), queries, key_rows, value_rows, out_grad)
    )


def solution(mesh):
    return jax.shard_map(
        per_device,
        mesh=mesh,
        in_specs=(P("ctx", "kvh"), P("ctx", "kvh"), P("ctx", "kvh"), P("ctx", "kvh"), P()),
        out_specs=(P(("ctx", "kvh"), None), P(("ctx", "kvh"), None), P(("ctx", "kvh"), None)),
        check_vma=False,
    )
```

time: 588 us -> 141 us (0.24)
  the two profiles are of different devices: /device:TPU:8 before, /device:TPU:1 now
where the time goes in v2:
time: 141 us; the launch traced here: 140 us
  Pallas kernels  134 us (95%)
  local copies, waits for them, and re-layouts  5.78 us (4%)
    pallas_call x1, Pallas kernels, per_device(): pl.pallas_call(kernel, out_shape=[jax.ShapeDtypeStruct((height, SIDE * wi...  134 us
    unnamed x8, local copies, waits for them, and re-layouts  5.08 us

profile of v2, /device:TPU:1, one launch (start us, length us, event | category | flops | bytes accessed | tf_op | source)
XLA Modules:
  0.0 140.4 jit_solution(5099265346886964072)
XLA Ops:
  0.6 0.8 copy.8
  1.4 0.7 reshape.9.picked
  2.1 134.0 %attend.1 = (bf16[384,2048]{1,0:T(8,128)(2,1)}, bf16[384,512]{1,0:T(8,128)(2,1)}, bf16[384,512]{1,0:T(8,128)(2,1)}) custom-call(s32[192]{0:T(256)} %reshape.9.picked, bf16[1536,512]{1,0:T(8,128)(2,1)} %queries.1, bf16[1536,128]{1,0:T(8,128)(2,1)} %keys.1, bf16[1536,128]{1,0:T(8,128)(2,1)} %values.1, bf16[1536,512]{1,0:T(8,128)(2,1)} %out_grad.1), custom_call_target="tpu_custom_call" | custom-call | tf_op jit(solution)/shard_map/attend/pallas_call | solution.py:532
  136.1 0.0 copy-start.1
  136.1 0.0 copy-start
  136.1 2.8 %copy.12 = bf16[384,2048]{1,0:T(8,128)(2,1)} copy(bf16[384,2048]{1,0:T(8,128)(2,1)} %get-tuple-element.6) | data formatting | bytes 3145728
  138.9 0.0 copy-done.1
  138.9 0.7 copy.13
  139.6 0.0 copy-done
  139.6 0.7 copy.14
Async XLA Ops:
  136.1 2.8 %copy-start.1 = (bf16[384,512]{1,0:T(8,128)(2,1)S(1)}, bf16[384,512]{1,0:T(8,128)(2,1)}, u32[]{:S(2)}) copy-start(bf16[384,512]{1,0:T(8,128)(2,1)} %get-tuple-element.7) | copy-start | bytes 1179652
  136.1 3.6 %copy-start = (bf16[384,512]{1,0:T(8,128)(2,1)S(1)}, bf16[384,512]{1,0:T(8,128)(2,1)}, u32[]{:S(2)}) copy-start(bf16[384,512]{1,0:T(8,128)(2,1)} %get-tuple-element.8) | copy-start | bytes 1179652

commit v3 on v2

--- a/solution.py
+++ b/solution.py
@@ -67,47 +67,95 @@
     )
 
 
-def head_step(query, grad, keys, values, live, tile):
-    weights_low = [[], [], []]
-    score_grads = [[], [], []]
+TILE = 256
+LOG_SCALE = SCALE * LOG2E
+
+
+def corner_scores(key, query, seen):
+    scores = dot(key[:seen], query, 1, 1)
+    key_at = lax.broadcasted_iota(jnp.int32, (TILE, TILE), 0)
+    row_at = lax.broadcasted_iota(jnp.int32, (TILE, TILE), 1)
+    corner = jnp.where(key_at <= row_at, scores[seen - TILE :], -BIG)
+    return corner if seen == TILE else jnp.concatenate([scores[: seen - TILE], corner], 0)
+
+
+def column_sum(values):
+    return jnp.sum(values, axis=0, keepdims=True)
+
+
+def own_totals(query, grad, key, value, stats, k):
+    for r in range(BLK // TILE):
+        rows = slice(r * TILE, (r + 1) * TILE)
+        seen = (r + 1) * TILE
+        scores = corner_scores(key, query[rows], seen)
+        weight_grads = dot(value[:seen], grad[rows], 1, 1)
+        top = jnp.max(scores, axis=0, keepdims=True) * LOG_SCALE
+        powers = jnp.exp2(scores * LOG_SCALE - top)
+        stats[k, 0:1, rows] = top
+        stats[k, 1:2, rows] = column_sum(powers)
+        stats[k, 2:3, rows] = column_sum(powers * weight_grads)
+
+
+def pick_step(query, grad, keys, values, live, stats, k):
+    weights_low = [[], []]
+    score_grads = [[], []]
     query_grads = []
-    for r in range(BLK // tile):
-        rows = slice(r * tile, (r + 1) * tile)
-        seen = (r + 1) * tile
-        ks = [keys[0][:seen], keys[1], keys[2]]
-        vs = [values[0][:seen], values[1], values[2]]
-        scores = [dot(k, query[rows], 1, 1) for k in ks]
-        key_at = lax.broadcasted_iota(jnp.int32, (tile, tile), 0)
-        row_at = lax.broadcasted_iota(jnp.int32, (tile, tile), 1)
-        corner = jnp.where(key_at <= row_at, scores[0][seen - tile :], -BIG)
-        scores[0] = corner if r == 0 else jnp.concatenate([scores[0][: seen - tile], corner], 0)
-        weight_grads = [dot(v, grad[rows], 1, 1) for v in vs]
-        tops = [jnp.max(s, axis=0, keepdims=True) for s in scores]
-        top = tops[0]
-        for j in (1, 2):
-            top = jnp.maximum(top, jnp.where(live[j], tops[j], -BIG))
-        top = top * (SCALE * LOG2E)
-        shifts = [top] + [jnp.where(live[j], top, BIG) for j in (1, 2)]
-        powers = [jnp.exp2(s * (SCALE * LOG2E) - h) for s, h in zip(scores, shifts)]
-        total = sum(jnp.sum(p, axis=0, keepdims=True) for p in powers)
-        mixed = sum(jnp.sum(p * w, axis=0, keepdims=True) for p, w in zip(powers, weight_grads))
+    for r in range(BLK // TILE):
+        rows = slice(r * TILE, (r + 1) * TILE)
+        scores = [dot(key, query[rows], 1, 1) for key in keys]
+        weight_grads = [dot(value, grad[rows], 1, 1) for value in values]
+        own_top = stats[k, 0:1, rows]
+        top = own_top
+        for j in range(2):
+            pick_top = jnp.max(scores[j], axis=0, keepdims=True) * LOG_SCALE
+            top = jnp.maximum(top, jnp.where(live[j], pick_top, -BIG))
+        shifts = [jnp.where(live[j], top, BIG) for j in range(2)]
+        powers = [jnp.exp2(s * LOG_SCALE - h) for s, h in zip(scores, shifts)]
+        own_part = jnp.exp2(own_top - top)
+        total = stats[k, 1:2, rows] * own_part + column_sum(powers[0]) + column_sum(powers[1])
+        mixed = stats[k, 2:3, rows] * own_part
+        for p, w in zip(powers, weight_grads):
+            mixed += column_sum(p * w)
         inverse = 1.0 / total
         delta = mixed * inverse
+        stats[k, 0:1, rows] = top
+        stats[k, 1:2, rows] = inverse
+        stats[k, 2:3, rows] = delta
         weights = [p * inverse for p in powers]
         grads = [(p * (w - delta)).astype(LOW) for p, w in zip(weights, weight_grads)]
-        query_grad = sum(dot(d, k, 0, 0) for d, k in zip(grads, ks))
-        query_grads.append((query_grad * SCALE).astype(LOW))
-        blank = jnp.zeros((BLK - seen, tile), LOW)
-        for j in range(3):
-            low = weights[j].astype(LOW)
-            pad = j == 0 and seen < BLK
-            weights_low[j].append(jnp.concatenate([low, blank], 0) if pad else low)
-            score_grads[j].append(jnp.concatenate([grads[j], blank], 0) if pad else grads[j])
+        query_grads.append(dot(grads[0], keys[0], 0, 0) + dot(grads[1], keys[1], 0, 0))
+        for j in range(2):
+            weights_low[j].append(weights[j].astype(LOW))
+            score_grads[j].append(grads[j])
     key_grads = [dot(jnp.concatenate(d, 1), query, 1, 0) for d in score_grads]
     value_grads = [dot(jnp.concatenate(w, 1), grad, 1, 0) for w in weights_low]
     return jnp.concatenate(query_grads, 0), key_grads, value_grads
 
 
+def own_step(query, grad, key, value, query_part, stats, k):
+    weights_low = []
+    score_grads = []
+    query_grads = []
+    for r in range(BLK // TILE):
+        rows = slice(r * TILE, (r + 1) * TILE)
+        seen = (r + 1) * TILE
+        scores = corner_scores(key, query[rows], seen)
+        weight_grads = dot(value[:seen], grad[rows], 1, 1)
+        weights = jnp.exp2(scores * LOG_SCALE - stats[k, 0:1, rows]) * stats[k, 1:2, rows]
+        low = weights.astype(LOW)
+        grads = (weights * (weight_grads - stats[k, 2:3, rows])).astype(LOW)
+        query_grads.append(((query_part[rows] + dot(grads, key[:seen], 0, 0)) * SCALE).astype(LOW))
+        if seen < BLK:
+            blank = jnp.zeros((BLK - seen, TILE), LOW)
+            low = jnp.concatenate([low, blank], 0)
+            grads = jnp.concatenate([grads, blank], 0)
+        weights_low.append(low)
+        score_grads.append(grads)
+    key_grad = dot(jnp.concatenate(score_grads, 1), query, 1, 0)
+    value_grad = dot(jnp.concatenate(weights_low, 1), grad, 1, 0)
+    return jnp.concatenate(query_grads, 0), key_grad, value_grad
+
+
 def second_of(block, c):
     return ((block // ROW) % 4) * (1 - c) + (block // LINE) * c
 
@@ -119,7 +167,7 @@
 
 def kernel(
     picked, queries, keys, values, out_grad, query_out, key_out, value_out,
-    query_v, grad_v, query_grad, pair, near, give, chosen, acc, own, own_far, other_part,
+    query_v, grad_v, query_grad, query_part, stats, pair, near, give, chosen, acc, own, own_far, other_part,
     sums, to_first, from_first, home, done, landed, at_home,
     sends, recvs, query_sems, query_recvs, final_sends, final_recvs, local_sems,
     *rounds,
@@ -166,6 +214,19 @@
     ]
     copies[3].start()
     copies[2].start()
+
+    def spots(r, h):
+        rows = pl.ds(pl.multiple_of(r * BLK, BLK), BLK)
+        return rows, pl.ds(pl.multiple_of(h * HEAD, HEAD), HEAD)
+
+    def totals(k, _):
+        rows, columns = spots(k // 4, k % 4)
+        own_totals(query_v[rows, columns], grad_v[rows, columns], keys[rows], values[rows], stats, k)
+        return 0
+
+    for load in loads:
+        load.wait()
+    lax.fori_loop(0, 4, totals, 0)
     copies[0].wait_recv()
     below = near.at[pl.ds(((a + 3) % 4) * ROW + c * 3, 3)]
     copies.append(remote(below, below, sends, recvs, 5, up))
@@ -192,6 +253,7 @@
                     again = jnp.logical_or(blocks[s] == blocks[0], blocks[s] == blocks[1])
                     known = jnp.logical_and(known, jnp.logical_not(again))
                 at_home[(r * 4 + o) * 4 + s] = jnp.where(known, near_at(blocks[s], c), -1)
+    lax.fori_loop(4, 12, totals, 0)
     for k in (1, 2, 4, 5):
         copies[k].wait_recv()
 
@@ -229,6 +291,8 @@
     def take_round(r):
         for m in (2, 3, 4, 5):
             flow(r, m).wait_recv()
+        if r == 0:
+            send_round(1)
 
         def pick(core, j):
             k = core * 2 + j
@@ -252,7 +316,7 @@
     def give_round(r):
         for j in range(2):
             for role in range(2):
-                value = acc[1 + j, role] * SCALE if role == 0 else acc[1 + j, role]
+                value = acc[j, role] * SCALE if role == 0 else acc[j, role]
                 low = value.astype(LOW)
 
                 @pl.when(c == role)
@@ -303,79 +367,69 @@
         parts[r][4] = blank
         merged[r][4] = blank
         came[r][12] = blank
-    for load in loads:
-        load.wait()
     relay_round(0)
     take_round(0)
     chosen_copy(0).wait_recv()
 
     for r in range(3):
-        if r < 2:
-            send_round(r + 1)
         acc[...] = jnp.zeros_like(acc)
         rows = pl.ds(r * BLK, BLK)
         block = index * 3 + r
-        live = (True, picked[2 * block] != block, picked[2 * block + 1] != block)
+        live = (picked[2 * block] != block, picked[2 * block + 1] != block)
 
         def body(h, _):
             @pl.when(h == 1)
             def _():
-                if r < 2:
-                    relay_round(r + 1)
+                if r == 0:
+                    relay_round(1)
+                    send_round(2)
                 if r > 0:
                     back_round(r - 1)
-
-            @pl.when(h == 2)
-            def _():
-                if r > 0:
-                    back_relay(r - 1)
 
             @pl.when(h == 3)
             def _():
                 if r < 2:
                     take_round(r + 1)
+                if r > 0:
+                    back_relay(r - 1)
 
             columns = pl.ds(pl.multiple_of(h * HEAD, HEAD), HEAD)
-            key_tiles = [keys[rows], chosen[4 * r], chosen[4 * r + 1]]
-            value_tiles = [values[rows], chosen[4 * r + 2], chosen[4 * r + 3]]
-            part, key_grads, value_grads = head_step(
-                query_v[rows, columns], grad_v[rows, columns], key_tiles, value_tiles, live, 256
+            part, key_grads, value_grads = pick_step(
+                query_v[rows, columns],
+                grad_v[rows, columns],
+                [chosen[4 * r], chosen[4 * r + 1]],
+                [chosen[4 * r + 2], chosen[4 * r + 3]],
+                live,
+                stats,
+                4 * r + h,
             )
-            query_grad[rows, columns] = part
-            for j in range(3):
+            query_part[rows, columns] = part
+            for j in range(2):
                 acc[j, 0] += key_grads[j]
                 acc[j, 1] += value_grads[j]
             return 0
 
+        if r == 1:
+            relay_round(2)
         lax.fori_loop(0, 4, body, 0)
-        own[0, r] = acc[0, 0] * SCALE
-        own[1, r] = acc[0, 1]
         give_round(r)
         if r < 2:
             chosen_copy(r + 1).wait_recv()
 
-    swap_own = remote(own.at[1 - c], own_far, sends, recvs, 49, sibling)
-    swap_own.start()
     height = query_out.shape[0]
     width = query_grad.shape[1]
-    query_columns = pl.ds(pl.multiple_of(z * width, HEAD), width)
+
+    def query_copy(h, o):
+        source = query_grad.at[pl.ds(((z + o) % SIDE) * height, height), spots(0, h)[1]]
+        target = query_out.at[:, pl.ds(pl.multiple_of(z * width + h * HEAD, HEAD), HEAD)]
+        if o == 0:
+            return pltpu.make_async_copy(source, target, local_sems.at[4 + h])
+        return remote(
+            source, target, query_sems, query_recvs, 3 * h + o - 1, (index, (z + o) % SIDE)
+        )
+
+    own[...] = jnp.zeros_like(own)
     back_round(2)
-    query_copies = []
-    for o in (2, 1, 3):
-        copy = remote(
-            query_grad.at[pl.ds(((z + o) % SIDE) * height, height)],
-            query_out.at[:, query_columns],
-            query_sems,
-            query_recvs,
-            o - 1,
-            (index, (z + o) % SIDE),
-        )
-        copy.start()
-        query_copies.append(copy)
-    stay = pltpu.make_async_copy(
-        query_grad.at[pl.ds(z * height, height)], query_out.at[:, query_columns], local_sems.at[0]
-    )
-    stay.start()
 
     def round_sum(r, t):
         total = None
@@ -389,63 +443,100 @@
             total = value if total is None else total + value
         return total
 
-    for r in (0, 1):
-        for m in (1, 3, 4, 5):
-            back_flow(r, m).wait_recv()
-
     def early(t, _):
         sums[t] = round_sum(0, t) + round_sum(1, t)
         return 0
-
-    lax.fori_loop(0, LINE // 2, early, 0)
-    back_relay(2)
-    lax.fori_loop(LINE // 2, LINE, early, 0)
-    swap_own.wait_recv()
-
-    def add_own(t, _):
-        sums[a * ROW + c * 3 + t] += own[c, t]
-        sums[a * ROW + (1 - c) * 3 + t] += own_far[t]
-        return 0
-
-    lax.fori_loop(0, 3, add_own, 0)
-    for m in (1, 3, 4, 5):
-        back_flow(2, m).wait_recv()
 
     def homeward(m):
         place_at = pl.ds(3 * m, 3)
         target = down if m in (1, 2, 5) else up
         return remote(to_first.at[place_at], from_first.at[place_at], sends, recvs, 50 + m, target)
 
-    for m, o, core in ((0, 2, 0), (2, 3, 0), (1, 2, 1), (3, 1, 1)):
-        start = ((a + o) % SIDE) * ROW + core * 3
-
-        def one(t, _):
-            to_first[3 * m + t] = (sums[start + t] + round_sum(2, start + t)).astype(LOW)
+    def send_home():
+        for m in (1, 3, 4, 5):
+            back_flow(2, m).wait_recv()
+        for m, o, core in ((0, 2, 0), (2, 3, 0), (1, 2, 1), (3, 1, 1)):
+            start = ((a + o) % SIDE) * ROW + core * 3
+
+            def one(t, _):
+                to_first[3 * m + t] = (sums[start + t] + round_sum(2, start + t)).astype(LOW)
+                return 0
+
+            lax.fori_loop(0, 3, one, 0)
+            homeward(m).start()
+        for o, core in ((1, 0), (3, 1)):
+            start = ((a + o) % SIDE) * ROW + core * 3
+
+            def ready(t, _):
+                sums[start + t] += round_sum(2, start + t)
+                return 0
+
+            lax.fori_loop(0, 3, ready, 0)
+
+    def relay_home():
+        for m, o, core in ((4, 1, 0), (5, 3, 1)):
+            start = ((a + o) % SIDE) * ROW + core * 3
+            homeward(m - 4).wait_recv()
+
+            def one(t, _):
+                to_first[3 * m + t] = (sums[start + t] + from_first[3 * (m - 4) + t].astype(F32)).astype(LOW)
+                return 0
+
+            lax.fori_loop(0, 3, one, 0)
+            homeward(m).start()
+
+    def tail(h, _):
+        @pl.when(h == 1)
+        def _():
+            back_relay(2)
+            for r in (0, 1):
+                for m in (1, 3, 4, 5):
+                    back_flow(r, m).wait_recv()
+            lax.fori_loop(0, LINE, early, 0)
+            send_home()
+
+        @pl.when(h == 3)
+        def _():
+            relay_home()
+
+        def one(r, _):
+            rows, columns = spots(r, h)
+            low, key_grad, value_grad = own_step(
+                query_v[rows, columns],
+                grad_v[rows, columns],
+                keys[rows],
+                values[rows],
+                query_part[rows, columns],
+                stats,
+                4 * r + h,
+            )
+            query_grad[rows, columns] = low
+            own[0, r] += key_grad * SCALE
+            own[1, r] += value_grad
             return 0
 
         lax.fori_loop(0, 3, one, 0)
-        homeward(m).start()
-    for m, o, core in ((4, 1, 0), (5, 3, 1)):
-        start = ((a + o) % SIDE) * ROW + core * 3
-
-        def ready(t, _):
-            sums[start + t] += round_sum(2, start + t)
-            return 0
-
-        def one(t, _):
-            to_first[3 * m + t] = (sums[start + t] + from_first[3 * (m - 4) + t].astype(F32)).astype(LOW)
-            return 0
-
-        lax.fori_loop(0, 3, ready, 0)
-        homeward(m - 4).wait_recv()
-        lax.fori_loop(0, 3, one, 0)
-        homeward(m).start()
+        for o in (2, 1, 3, 0):
+            query_copy(h, o).start()
+        return 0
+
+    lax.fori_loop(0, 4, tail, 0)
+    swap_own = remote(own.at[1 - c], own_far, sends, recvs, 49, sibling)
+    swap_own.start()
 
     def stays(t, _):
         home[t] = sums[a * ROW + t] + round_sum(2, a * ROW + t)
         return 0
 
     lax.fori_loop(0, ROW, stays, 0)
+    swap_own.wait_recv()
+
+    def add_own(t, _):
+        home[c * 3 + t] += own[c, t]
+        home[(1 - c) * 3 + t] += own_far[t]
+        return 0
+
+    lax.fori_loop(0, 3, add_own, 0)
 
     finals = []
     columns = pl.ds(pl.multiple_of(z * HEAD, HEAD), HEAD)
@@ -506,9 +597,9 @@
     ).wait_recv()
     key_out[...] = landed[0]
     value_out[...] = landed[1]
-    for copy in query_copies:
-        copy.wait()
-    stay.wait()
+    for h in range(4):
+        for o in range(4):
+            query_copy(h, o).wait()
     ends = [swap, swap_own] + copies + finals + [cross] + [homeward(m) for m in range(6)]
     for r in range(3):
         ends += [chosen_copy(r), part_copy(r)]
@@ -542,11 +633,13 @@
                 pltpu.VMEM((tokens, width), LOW),
                 pltpu.VMEM((tokens, width), LOW),
                 pltpu.VMEM((tokens, width), LOW),
+                pltpu.VMEM((tokens, width), F32),
+                pltpu.VMEM((12, 8, BLK), F32),
                 pltpu.VMEM((2, 3) + tile, LOW),
                 blocks(LINE),
                 blocks(6),
                 blocks(12),
-                pltpu.VMEM((3, 2) + tile, F32),
+                pltpu.VMEM((2, 2) + tile, F32),
                 pltpu.VMEM((2, 3) + tile, F32),
                 blocks(3, F32),
                 blocks(6),
@@ -559,11 +652,11 @@
                 pltpu.SMEM((48,), jnp.int32),
                 dma((56,)),
                 dma((56,)),
-                dma((3,)),
-                dma((3,)),
+                dma((12,)),
+                dma((12,)),
                 dma((2, 4)),
                 dma((2, 4)),
-                dma((4,)),
+                dma((8,)),
             ]
             + [blocks(12)] * 6
             + [blocks(5)] * 6

time: 141 us -> 127 us (0.901)
  Pallas kernels: 134 us -> 120 us
    pallas_call x1, Pallas kernels: 134 us -> 120 us  [per_device(): pl.pallas_call(kernel, out_shape=[jax.ShapeDtypeStruct((height, SIDE * wi...]
where the time goes in v3:
time: 127 us; the launch traced here: 126 us
  Pallas kernels  120 us (94%)
  local copies, waits for them, and re-layouts  5.78 us (5%)
    pallas_call x1, Pallas kernels, per_device(): pl.pallas_call(kernel, out_shape=[jax.ShapeDtypeStruct((height, SIDE * wi...  120 us
    unnamed x8, local copies, waits for them, and re-layouts  5.08 us

profile of v3, /device:TPU:1, one launch (start us, length us, event | category | flops | bytes accessed | tf_op | source)
XLA Modules:
  0.0 126.4 jit_solution(3531684986341800125)
XLA Ops:
  0.6 0.8 copy.8
  1.4 0.7 reshape.9.picked
  2.1 120.0 %attend.1 = (bf16[384,2048]{1,0:T(8,128)(2,1)}, bf16[384,512]{1,0:T(8,128)(2,1)}, bf16[384,512]{1,0:T(8,128)(2,1)}) custom-call(s32[192]{0:T(256)} %reshape.9.picked, bf16[1536,512]{1,0:T(8,128)(2,1)} %queries.1, bf16[1536,128]{1,0:T(8,128)(2,1)} %keys.1, bf16[1536,128]{1,0:T(8,128)(2,1)} %values.1, bf16[1536,512]{1,0:T(8,128)(2,1)} %out_grad.1), custom_call_target="tpu_custom_call" | custom-call | tf_op jit(solution)/shard_map/attend/pallas_call | solution.py:623
  122.1 0.0 copy-start.1
  122.1 0.0 copy-start
  122.1 2.8 %copy.12 = bf16[384,2048]{1,0:T(8,128)(2,1)} copy(bf16[384,2048]{1,0:T(8,128)(2,1)} %get-tuple-element.6) | data formatting | bytes 3145728
  124.9 0.0 copy-done.1
  124.9 0.7 copy.13
  125.7 0.0 copy-done
  125.7 0.7 copy.14
Async XLA Ops:
  122.1 2.8 %copy-start.1 = (bf16[384,512]{1,0:T(8,128)(2,1)S(1)}, bf16[384,512]{1,0:T(8,128)(2,1)}, u32[]{:S(2)}) copy-start(bf16[384,512]{1,0:T(8,128)(2,1)} %get-tuple-element.7) | copy-start | bytes 1179652
  122.1 3.6 %copy-start = (bf16[384,512]{1,0:T(8,128)(2,1)S(1)}, bf16[384,512]{1,0:T(8,128)(2,1)}, u32[]{:S(2)}) copy-start(bf16[384,512]{1,0:T(8,128)(2,1)} %get-tuple-element.8) | copy-start | bytes 1179652

commit v4 on v3

--- a/solution.py
+++ b/solution.py
@@ -58,7 +58,7 @@
     barrier = pltpu.get_barrier_semaphore()
     for device in devices:
         pl.semaphore_signal(barrier, inc=1, device_id=device, device_id_type=MESH)
-    pl.semaphore_wait(barrier, len(devices))
+    return lambda: pl.semaphore_wait(barrier, len(devices))
 
 
 def dot(left, right, left_dim, right_dim):
@@ -183,6 +183,7 @@
     seconds = {o: on_second(x, y, c, z, o) for o in (1, 2, 3)}
     depth = {(k, o): (here + k, (z + o) % SIDE) for k in (0, 1) for o in (1, 2, 3)}
     up, down = firsts[1], firsts[3]
+    all_here = greet([sibling, up, down, seconds[1], seconds[3]] + list(depth.values()))
 
     loads = [
         pltpu.make_async_copy(queries, query_v, local_sems.at[2]),
@@ -195,7 +196,7 @@
         pair[1, t] = values[t * BLK : (t + 1) * BLK]
     for t in range(3):
         near[a * ROW + c * 3 + t] = pair[c, t]
-    greet([sibling, up, down, seconds[1], seconds[3]] + list(depth.values()))
+    all_here()
 
     mine = near.at[pl.ds(a * ROW + c * 3, 3)]
     theirs = near.at[pl.ds(a * ROW + (1 - c) * 3, 3)]
@@ -431,7 +432,7 @@
     own[...] = jnp.zeros_like(own)
     back_round(2)
 
-    def round_sum(r, t):
+    def round_sum(r, t, rows=pl.ds(0, BLK)):
         total = None
         for o in range(4):
             start = (r * 4 + o) * 4
@@ -439,7 +440,7 @@
             spot = 4 if o == 0 else 12
             for s in (3, 2, 1, 0):
                 spot = jnp.where(at_home[start + s] == t, base + s, spot)
-            value = (merged[r] if o == 0 else came[r])[spot].astype(F32)
+            value = (merged[r] if o == 0 else came[r])[spot, rows].astype(F32)
             total = value if total is None else total + value
         return total
 
@@ -447,43 +448,31 @@
         sums[t] = round_sum(0, t) + round_sum(1, t)
         return 0
 
-    def homeward(m):
-        place_at = pl.ds(3 * m, 3)
-        target = down if m in (1, 2, 5) else up
-        return remote(to_first.at[place_at], from_first.at[place_at], sends, recvs, 50 + m, target)
-
-    def send_home():
-        for m in (1, 3, 4, 5):
-            back_flow(2, m).wait_recv()
-        for m, o, core in ((0, 2, 0), (2, 3, 0), (1, 2, 1), (3, 1, 1)):
-            start = ((a + o) % SIDE) * ROW + core * 3
-
-            def one(t, _):
-                to_first[3 * m + t] = (sums[start + t] + round_sum(2, start + t)).astype(LOW)
-                return 0
-
-            lax.fori_loop(0, 3, one, 0)
-            homeward(m).start()
-        for o, core in ((1, 0), (3, 1)):
-            start = ((a + o) % SIDE) * ROW + core * 3
-
-            def ready(t, _):
-                sums[start + t] += round_sum(2, start + t)
-                return 0
-
-            lax.fori_loop(0, 3, ready, 0)
-
-    def relay_home():
-        for m, o, core in ((4, 1, 0), (5, 3, 1)):
-            start = ((a + o) % SIDE) * ROW + core * 3
-            homeward(m - 4).wait_recv()
-
-            def one(t, _):
-                to_first[3 * m + t] = (sums[start + t] + from_first[3 * (m - 4) + t].astype(F32)).astype(LOW)
-                return 0
-
-            lax.fori_loop(0, 3, one, 0)
-            homeward(m).start()
+    half = BLK // 2
+    halves = (pl.ds(0, half), pl.ds(half, half))
+    plans = ((2, 0), (2, 1), (1, 1), (3, 0), (1, 0), (3, 1))
+
+    def homeward(k, m):
+        target = down if m in (1, 3, 5) else up
+        return remote(
+            to_first.at[6 * k + m], from_first.at[6 * k + m], sends, recvs, 50 + 6 * k + m, target
+        )
+
+    def send_home(k, m):
+        o, side = plans[m]
+        start = ((a + o) % SIDE) * ROW + k * 3
+        if m >= 4:
+            homeward(k, m - 4).wait_recv()
+
+        def one(t, _):
+            total = sums[start + t, halves[side]] + round_sum(2, start + t, halves[side])
+            if m >= 4:
+                total += from_first[6 * k + m - 4, t].astype(F32)
+            to_first[6 * k + m, t] = total.astype(LOW)
+            return 0
+
+        lax.fori_loop(0, 3, one, 0)
+        homeward(k, m).start()
 
     def tail(h, _):
         @pl.when(h == 1)
@@ -493,11 +482,20 @@
                 for m in (1, 3, 4, 5):
                     back_flow(r, m).wait_recv()
             lax.fori_loop(0, LINE, early, 0)
-            send_home()
+            for m in (1, 3, 4, 5):
+                back_flow(2, m).wait_recv()
+            for k, m in ((0, 0), (0, 1), (0, 2), (0, 3), (1, 0), (1, 1)):
+                send_home(k, m)
+
+        @pl.when(h == 2)
+        def _():
+            for k, m in ((0, 4), (0, 5), (1, 2), (1, 3)):
+                send_home(k, m)
 
         @pl.when(h == 3)
         def _():
-            relay_home()
+            for m in (4, 5):
+                send_home(1, m)
 
         def one(r, _):
             rows, columns = spots(r, h)
@@ -541,14 +539,16 @@
     finals = []
     columns = pl.ds(pl.multiple_of(z * HEAD, HEAD), HEAD)
     for k in (0, 1):
-        for m in (2 + k, 4 + k):
-            homeward(m).wait_recv()
+        for m in (2, 3, 4, 5):
+            homeward(k, m).wait_recv()
 
         def finish(t, _):
-            total = home[k * 3 + t]
-            for m in (2 + k, 4 + k):
-                total += from_first[3 * m + t].astype(F32)
-            done[k, pl.ds(pl.multiple_of(t * BLK, BLK), BLK)] = total.astype(LOW)
+            for side, pair_of in ((0, (3, 4)), (1, (2, 5))):
+                total = home[k * 3 + t, halves[side]]
+                for m in pair_of:
+                    total += from_first[6 * k + m, t].astype(F32)
+                rows = pl.ds(pl.multiple_of(t * BLK + side * half, half), half)
+                done[k, rows] = total.astype(LOW)
             return 0
 
         lax.fori_loop(0, 3, finish, 0)
@@ -600,7 +600,7 @@
     for h in range(4):
         for o in range(4):
             query_copy(h, o).wait()
-    ends = [swap, swap_own] + copies + finals + [cross] + [homeward(m) for m in range(6)]
+    ends = [swap, swap_own] + copies + finals + [cross] + [homeward(k, m) for k in (0, 1) for m in range(6)]
     for r in range(3):
         ends += [chosen_copy(r), part_copy(r)]
         ends += [flow(r, m) for m in range(6)] + [back_flow(r, m) for m in range(6)]
@@ -644,14 +644,14 @@
                 blocks(3, F32),
                 blocks(6),
                 blocks(LINE, F32),
-                blocks(3 * ROW),
-                blocks(3 * ROW),
+                pltpu.VMEM((12, 3, BLK // 2, HEAD), LOW),
+                pltpu.VMEM((12, 3, BLK // 2, HEAD), LOW),
                 blocks(ROW, F32),
                 pltpu.VMEM((2, 3 * BLK, HEAD), LOW),
                 pltpu.VMEM((2, height, SIDE * HEAD), LOW),
                 pltpu.SMEM((48,), jnp.int32),
-                dma((56,)),
-                dma((56,)),
+                dma((62,)),
+                dma((62,)),
                 dma((12,)),
                 dma((12,)),
                 dma((2, 4)),

time: 127 us -> 126 us (level)
  no operation moved by 1% of the time
where the time goes in v4:
time: 126 us
  Pallas kernels  119 us (94%)
  local copies, waits for them, and re-layouts  5.78 us (5%)
    pallas_call x1, Pallas kernels, per_device(): pl.pallas_call(kernel, out_shape=[jax.ShapeDtypeStruct((height, SIDE * wi...  119 us
    unnamed x8, local copies, waits for them, and re-layouts  5.08 us

profile of v4, /device:TPU:1, one launch (start us, length us, event | category | flops | bytes accessed | tf_op | source)
XLA Modules:
  0.0 125.7 jit_solution(15602822256184488193)
XLA Ops:
  0.6 0.8 copy.8
  1.4 0.7 reshape.9.picked
  2.1 119.3 %attend.1 = (bf16[384,2048]{1,0:T(8,128)(2,1)}, bf16[384,512]{1,0:T(8,128)(2,1)}, bf16[384,512]{1,0:T(8,128)(2,1)}) custom-call(s32[192]{0:T(256)} %reshape.9.picked, bf16[1536,512]{1,0:T(8,128)(2,1)} %queries.1, bf16[1536,128]{1,0:T(8,128)(2,1)} %keys.1, bf16[1536,128]{1,0:T(8,128)(2,1)} %values.1, bf16[1536,512]{1,0:T(8,128)(2,1)} %out_grad.1), custom_call_target="tpu_custom_call" | custom-call | tf_op jit(solution)/shard_map/attend/pallas_call | solution.py:623
  121.4 0.0 copy-start.1
  121.4 0.0 copy-start
  121.4 2.8 %copy.12 = bf16[384,2048]{1,0:T(8,128)(2,1)} copy(bf16[384,2048]{1,0:T(8,128)(2,1)} %get-tuple-element.6) | data formatting | bytes 3145728
  124.2 0.0 copy-done.1
  124.2 0.7 copy.13
  125.0 0.0 copy-done
  125.0 0.7 copy.14
Async XLA Ops:
  121.4 2.8 %copy-start.1 = (bf16[384,512]{1,0:T(8,128)(2,1)S(1)}, bf16[384,512]{1,0:T(8,128)(2,1)}, u32[]{:S(2)}) copy-start(bf16[384,512]{1,0:T(8,128)(2,1)} %get-tuple-element.7) | copy-start | bytes 1179652
  121.4 3.6 %copy-start = (bf16[384,512]{1,0:T(8,128)(2,1)S(1)}, bf16[384,512]{1,0:T(8,128)(2,1)}, u32[]{:S(2)}) copy-start(bf16[384,512]{1,0:T(8,128)(2,1)} %get-tuple-element.8) | copy-start | bytes 1179652
